TPU v7x, 256 devices: a whole 4x4x8 slice. The times are simulated.
256 devices in a mesh: row: 16 (over z_hi, y, core), col: 16 (over z_lo, x).
Axes of the slice: x: 4, y: 4, z: 8 (z_hi: 2, z_lo: 4; z = z_hi * 4 + z_lo), core: 2. Of those that a mesh axis runs over, the one named last changes fastest.
Arguments:
- tensor: float32 [32, 4096, 4096], P(None, 'row', 'col'), may hold values from -120 to 120
- factor_b: float32 [4096, 256], P('col', 'row'), may hold values from -1 to 1
- factor_c: float32 [32, 256], replicated, may hold values from -5 to 5
Outputs:
- factor_a: float32 [4096, 256], P(('row', 'col'))
- col_scale: float32 [256], replicated
All inputs are finite; a program needn't handle non-finite values.
Results may differ from a plain program's by a relative error of at most 0.0003.
Values sent between devices are 32-bit elements; how exact they have to be, the bound alone decides.
No kernel may reach another device: no remote copies, remote signals or barrier semaphores. Data moves between devices by JAX's collectives and lax.ppermute only.
A program may use at most 64 MiB of HBM per device.

v0:
```python
import jax
import jax.numpy as jnp
from jax import lax
from jax.sharding import PartitionSpec as P

eps = 1e-06


def contract_rows(slab, block_b, factor_c, high):
    depth, count, cols_j = slab.shape
    product = jnp.dot(
        slab.reshape(depth * count, cols_j),
        block_b,
        precision=high,
        preferred_element_type=jnp.float32,
    )
    product = product.reshape(depth, count, block_b.shape[1])
    return jnp.sum(product * factor_c[:, None, :], axis=0)


def sum_gram(partial_gram):
    return lax.psum(partial_gram, "col")


def local(tensor, factor_b, factor_c):
    high = lax.Precision.HIGHEST
    depth, rows_i, cols_j = tensor.shape
    block_b = lax.all_gather(factor_b, "row", axis=1, tiled=True)
    partial_gram = jnp.dot(block_b.T, block_b, precision=high, preferred_element_type=jnp.float32)
    gram_c = jnp.dot(factor_c.T, factor_c, precision=high, preferred_element_type=jnp.float32)
    share = rows_i // lax.axis_size("col")
    local_terms = contract_rows(tensor, block_b, factor_c, high)
    gram_b = sum_gram(partial_gram)
    summed = lax.psum(local_terms, "col")
    mine = lax.dynamic_slice_in_dim(summed, lax.axis_index("col") * share, share, 0)
    gram = gram_b * gram_c
    lower = jnp.linalg.cholesky(gram)
    half = lax.linalg.triangular_solve(lower, mine, left_side=False, lower=True, transpose_a=True)
    solved = lax.linalg.triangular_solve(
        lower, half, left_side=False, lower=True, transpose_a=False
    )
    squares = lax.psum(jnp.sum(solved * solved, axis=0), ("row", "col"))
    col_scale = jnp.sqrt(squares / (rows_i * lax.axis_size("row")) + eps)
    return (solved / col_scale, col_scale)


def solution(mesh):
    return jax.shard_map(
        local,
        mesh=mesh,
        in_specs=(P(None, "row", "col"), P("col", "row"), P()),
        out_specs=(P(("row", "col"), None), P()),
        check_vma=False,
    )
```

profile of v0, /device:TPU:1, one launch (start us, length us, event | category | flops | bytes accessed | tf_op | source)
XLA Modules:
  0.0 357.1 jit_solution(18430025002695049809)
XLA Ops:
  7.2 0.0 copy-start
  7.2 0.0 all-reduce.4.cloned.1.call-start
  7.2 35.7 %all_gather.3 = f32[256,256]{0,1:T(8,128)S(1)} all-gather(f32[256,16]{0,1:T(8,128)} %param.4), channel_id=1, replica_groups=mesh['row'=16,'col'=16] {'row'}, dimensions={1}, use_global_device_ids=true | all-gather | bytes 278528 | tf_op jit(solution)/shard_map/all_gather | solution.py:28
  42.9 1.1 fusion.15
  44.0 10.1 %multiply_reduce_fusion = f32[256,256]{1,0:T(8,128)} fusion(f32[32,256]{1,0:T(8,128)} %param.5, f32[32,256,256]{2,1,0:T(8,128)} %param.3, f32[256,256]{0,1:T(8,128)S(1)} %all_gather.3), kind=kOutput, calls=%fused_computation.2 | convolution fusion | flops 6446579712 | bytes 8945664 | tf_op jit(solution)/shard_map/dot_general | solution.py:11
  54.1 0.0 all-reduce.4.cloned.1.call-update
  54.1 146.1 %all-reduce.4.cloned.1.call-done = (f32[256,256]{0,1:T(8,128)}, f32[256,256]{1,0:T(8,128)}) async-done(((f32[256,256]{0,1:T(8,128)}, f32[256,256]{1,0:T(8,128)}), (f32[256,256]{0,1:T(8,128)}, f32[256,256]{1,0:T(8,128)})) %all-reduce.4.cloned.1.call-update) | async-done | bytes 524304 | tf_op jit(solution)/shard_map/psum | solution.py:22
  200.2 0.0 copy-done
  200.2 1.4 convolution_multiply_fusion
  201.5 0.1 copy.7
  201.7 11.7 %cholesky.50 = f32[128,128]{1,0:T(8,128)S(1)} custom-call(f32[128,128]{1,0:T(8,128)S(1)} %cholesky.118), custom_call_target="Cholesky" | custom-call | tf_op jit(solution)/shard_map/jit(cholesky)/cholesky | solution.py:37
  213.5 9.8 %custom-call.16 = f32[1,128,128]{1,2,0:T(8,128)S(1)} custom-call(f32[1,128,128]{2,1,0:T(8,128)S(1)} %get-tuple-element.25), custom_call_target="InvertDiagBlocksLowerTriangular" | custom-call | tf_op jit(solution)/shard_map/jit(cholesky)/cholesky | solution.py:37
  223.3 0.2 constant_dynamic-update-slice_fusion.1
  223.5 0.3 convolution_subtract_fusion
  223.8 11.7 %cholesky.105 = f32[128,128]{1,0:T(8,128)S(1)} custom-call(f32[128,128]{1,0:T(8,128)S(1)} %convolution_subtract_fusion), custom_call_target="Cholesky" | custom-call | tf_op jit(solution)/shard_map/jit(cholesky)/cholesky | solution.py:37
  235.6 0.7 compare_reduce_fusion
  237.6 0.1 triangular_solve.67
  237.7 3.9 %while.1 = (s32[]{:T(128)}, f32[256,256]{1,0:T(8,128)S(1)}, s32[2,2]{1,0:T(2,128)S(1)}, f32[2,128,128]{2,1,0:T(8,128)S(1)}, s32[]{:T(128)}) while((s32[]{:T(128)}, f32[256,256]{1,0:T(8,128)S(1)}, s32[2,2]{1,0:T(2,128)S(1)}, f32[2,128,128]{2,1,0:T(8,128)S(1)}, s32[]{:T(128)}) %tuple.27), condition=%wide.while_cond, body=%wide.while_body.sunk | while | flops 2 | bytes 131181 | solution.py:38
  237.7 0.6 fusion.29
  238.2 1.4 bitcast_dynamic-update-slice_fusion.2
  239.6 0.6 fusion.29
  240.2 1.4 bitcast_dynamic-update-slice_fusion.2
  241.6 19.9 %custom-call.17 = f32[2,128,128]{1,2,0:T(8,128)S(1)} custom-call(f32[2,128,128]{2,1,0:T(8,128)S(1)} %get-tuple-element.9), custom_call_target="InvertDiagBlocksLowerTriangular" | custom-call | tf_op jit(solution)/shard_map/triangular_solve | solution.py:38
  261.5 0.9 fusion.6
  262.4 0.9 convolution_subtract_fusion.2
  263.2 0.2 fusion.8
  263.4 0.2 fusion.7
  263.6 0.2 convolution_subtract_fusion.1
  263.8 0.2 fusion.5
  264.0 0.1 multiply_reduce_fusion.1
  264.1 85.5 %psum.23 = f32[256]{0:T(256)S(1)} all-reduce(f32[256]{0:T(256)S(1)} %multiply_reduce_fusion.1), channel_id=1, replica_groups=mesh['row'=16,'col'=16] {'row','col'}, use_global_device_ids=true, to_apply=%region_8.9 | all-reduce | flops 256 | bytes 2048 | tf_op jit(solution)/shard_map/psum | solution.py:42
  349.6 0.6 fusion.11
  (13 shorter events, 0.2 us)
Async XLA Ops:
  7.2 193.0 %copy-start = (f32[32,256]{1,0:T(8,128)S(1)}, f32[32,256]{1,0:T(8,128)}, u32[]{:S(2)}) copy-start(f32[32,256]{1,0:T(8,128)} %param.5) | copy-start | bytes 98308
  7.2 193.0 %all-reduce.4.cloned.1.call-start = ((), (), s32[]{:S(2)}) async-start(), calls=%async_computation | async-start | bytes 1048576 | tf_op jit(solution)/shard_map/psum | solution.py:22
  349.6 0.6 copy-start.1
Sparse Core Ops, SparseCore 0:
  54.2 145.9 all-reduce.3
where the time goes:
time: 357 us
  waiting for transfers between devices  146 us (41%)
  blocking collectives  121 us (34%)
  other arithmetic  54.7 us (15%)
  matrix products  15.5 us (4%)
  between operations  15.4 us (4%)
  local copies, waits for them, and re-layouts  4.14 us (1%)
    psum x1, waiting for transfers between devices, sum_gram(): return lax.psum(partial_gram, 'col')  146 us
    psum x1, blocking collectives, local(): squares = lax.psum(jnp.sum(solved * solved, axis=0), ('row', 'col'))  85.5 us
    all_gather x1, blocking collectives, local(): block_b = lax.all_gather(factor_b, 'row', axis=1, tiled=True)  35.7 us
    another operation x6, other arithmetic, local(): lower = jnp.linalg.cholesky(gram)  34 us
    another operation x3, other arithmetic, local(): lax.linalg.triangular_solve(lower, mine, left_side=False, lower=True, tra...  19.9 us
    dot_general x1, matrix products, contract_rows(): jnp.dot(slab.reshape(depth * count, cols_j), block_b, precision=high, pre...  10.1 us
  transfers between devices with their start and end apart: 1, of which 1 were waited for; matrix products, arithmetic and copies ran while one was open for 0% of the time, Pallas kernels for 0%

commit v1 on v0

v1 whole, which is shorter than its diff:
```python
import jax
import jax.numpy as jnp
from jax import lax
from jax.sharding import PartitionSpec as P

eps = 1e-06


def gather_blocks(block, axis):
    count = lax.axis_size(axis)
    copies = jnp.broadcast_to(block[None], (count,) + block.shape)
    return lax.all_to_all(copies, axis, 0, 0)


def scatter_sum(whole, axis):
    count = lax.axis_size(axis)
    pieces = whole.reshape(count, whole.shape[0] // count, whole.shape[1])
    return jnp.sum(lax.all_to_all(pieces, axis, 0, 0), axis=0)


def contract_rows(slab, block_bt, factor_c):
    depth, count, cols_j = slab.shape
    product = lax.dot_general(
        slab.reshape(depth * count, cols_j),
        block_bt,
        (((1,), (1,)), ((), ())),
        precision=lax.Precision.HIGH,
        preferred_element_type=jnp.float32,
    )
    product = product.reshape(depth, count, block_bt.shape[0])
    return jnp.sum(product * factor_c[:, None, :], axis=0)


def local(tensor, factor_b, factor_c):
    high = lax.Precision.HIGHEST
    depth, rows_i, cols_j = tensor.shape
    ranks = factor_c.shape[1]
    block_bt = gather_blocks(factor_b.T, "row").reshape(ranks, cols_j)
    partial_gram = lax.dot_general(
        block_bt, block_bt, (((1,), (1,)), ((), ())), precision=high,
        preferred_element_type=jnp.float32,
    )
    gram_c = jnp.dot(factor_c.T, factor_c, precision=high, preferred_element_type=jnp.float32)
    gram_rows = scatter_sum(partial_gram, "col")
    gram_b = gather_blocks(gram_rows, "col").reshape(ranks, ranks)
    mine = scatter_sum(contract_rows(tensor, block_bt, factor_c), "col")
    gram = gram_b * gram_c
    lower = jnp.linalg.cholesky(gram)
    half = lax.linalg.triangular_solve(lower, mine, left_side=False, lower=True, transpose_a=True)
    solved = lax.linalg.triangular_solve(
        lower, half, left_side=False, lower=True, transpose_a=False
    )
    squares = gather_blocks(jnp.sum(solved * solved, axis=0)[None], ("row", "col"))
    squares = jnp.sum(squares[:, 0], axis=0)
    col_scale = jnp.sqrt(squares / (rows_i * lax.axis_size("row")) + eps)
    return (solved / col_scale, col_scale)


def solution(mesh):
    return jax.shard_map(
        local,
        mesh=mesh,
        in_specs=(P(None, "row", "col"), P("col", "row"), P()),
        out_specs=(P(("row", "col"), None), P()),
        check_vma=False,
    )
```

time: 357 us -> 159 us (0.45)
  waiting for transfers between devices: 146 us -> 19.2 us
  blocking collectives: 121 us -> 47.2 us
  starting transfers between devices: 0.04 us -> 18 us
  between operations: 15.4 us -> 2.16 us
  matrix products: 15.5 us -> 10.7 us
    psum x1 -> x0, waiting for transfers between devices: 146 us -> none  [sum_gram(): return lax.psum(partial_gram, 'col')]
    psum x1 -> x0, blocking collectives: 85.5 us -> none  [local(): squares = lax.psum(jnp.sum(solved * solved, axis=0), ('row', 'col'))]
    all_to_all x0 -> x2, blocking collectives: none -> 47.2 us  [gather_blocks(): return lax.all_to_all(copies, axis, 0, 0)]
    all_gather x1 -> x0, blocking collectives: 35.7 us -> none  [local(): block_b = lax.all_gather(factor_b, 'row', axis=1, tiled=True)]
    all_to_all x0 -> x3, waiting for transfers between devices: none -> 19.2 us  [the longest x2 10.4 us: scatter_sum(): return jnp.sum(lax.all_to_all(pieces, axis, 0, 0), axis=0)]
    all_to_all x0 -> x3, starting transfers between devices: none -> 18 us  [the longest x2 13.2 us: scatter_sum(): return jnp.sum(lax.all_to_all(pieces, axis, 0, 0), axis=0)]
  transfers between devices with their start and end apart: 1 -> 3, of which waited for: 1 -> 3; matrix products, arithmetic and copies ran while one was open for 0% -> 5% of each run, Pallas kernels for 0% -> 0%
where the time goes in v1:
time: 159 us; the launch traced here: 158 us
  other arithmetic  55 us (35%)
  blocking collectives  47.2 us (30%)
  waiting for transfers between devices  19.2 us (12%)
  starting transfers between devices  18 us (11%)
  matrix products  10.7 us (7%)
  local copies, waits for them, and re-layouts  6.02 us (4%)
  between operations  2.16 us (1%)
    all_to_all x2, blocking collectives, gather_blocks(): return lax.all_to_all(copies, axis, 0, 0)  47.2 us
    another operation x6, other arithmetic, local(): lower = jnp.linalg.cholesky(gram)  34 us
    another operation x3, other arithmetic, local(): lax.linalg.triangular_solve(lower, mine, left_side=False, lower=True, tra...  19.9 us
    all_to_all x2, starting transfers between devices, scatter_sum(): return jnp.sum(lax.all_to_all(pieces, axis, 0, 0), axis=0)  13.2 us
    all_to_all x2, waiting for transfers between devices, scatter_sum(): return jnp.sum(lax.all_to_all(pieces, axis, 0, 0), axis=0)  10.4 us
    all_to_all x1, waiting for transfers between devices, gather_blocks(): return lax.all_to_all(copies, axis, 0, 0)  8.78 us
    dot_general x1, matrix products, contract_rows(): lax.dot_general(slab.reshape(depth * count, cols_j), block_bt, (((1,), (1...  7.57 us
    all_to_all x1, starting transfers between devices, gather_blocks(): return lax.all_to_all(copies, axis, 0, 0)  4.77 us
  transfers between devices with their start and end apart: 3, of which 3 were waited for; matrix products, arithmetic and copies ran while one was open for 5% of the time, Pallas kernels for 0%

profile of v1, /device:TPU:1, one launch (start us, length us, event | category | flops | bytes accessed | tf_op | source)
XLA Modules:
  0.0 158.3 jit_solution(6584247313038032800)
XLA Ops:
  0.6 0.7 broadcast_in_dim.7
  1.4 23.5 %all_to_all.25 = f32[16,16,256]{2,1,0:T(8,128)S(1)} all-to-all(f32[16,16,256]{2,1,0:T(8,128)S(1)} %broadcast_in_dim.7), channel_id=1, replica_groups=mesh['row'=16,'col'=16] {'row'}, dimensions={0} | all-to-all | bytes 524288 | tf_op jit(solution)/shard_map/all_to_all | solution.py:12
  24.9 1.1 fusion.13
  26.0 7.8 %all-to-all-start.2 = ((f32[16,16,256]{2,1,0:T(8,128)}), f32[16,16,256]{2,1,0:T(8,128)S(1)}, u32[]{:S(2)}, u32[]{:S(2)}) async-start(f32[16,16,256]{2,1,0:T(8,128)} %fusion.13), calls=%async_computation.2 | async-start | bytes 524288 | tf_op jit(solution)/shard_map/all_to_all | solution.py:18
  33.8 7.6 %multiply_reduce_fusion = f32[256,256]{1,0:T(8,128)} fusion(f32[32,256]{1,0:T(8,128)} %param.5, f32[32,256,256]{2,1,0:T(8,128)} %param.3, f32[256,256,1]{1,0,2:T(8,128)S(1)} %bitcast.49), kind=kOutput, calls=%fused_computation.2 | convolution fusion | flops 3225354240 | bytes 8945664 | tf_op jit(solution)/shard_map/dot_general | solution.py:23
  41.4 1.6 all-to-all-done.2
  43.0 5.4 %all-to-all-start.1 = ((f32[16,16,256]{2,1,0:T(8,128)}), f32[16,16,256]{2,1,0:T(8,128)S(1)}, u32[]{:S(2)}, u32[]{:S(2)}) async-start(f32[16,16,256]{2,1,0:T(8,128)} %bitcast.3), calls=%async_computation.1 | async-start | bytes 524288 | tf_op jit(solution)/shard_map/all_to_all | solution.py:18
  48.4 8.8 %all-to-all-done.1 = f32[16,16,256]{2,1,0:T(8,128)S(1)} async-done(((f32[16,16,256]{2,1,0:T(8,128)}), f32[16,16,256]{2,1,0:T(8,128)S(1)}, u32[]{:S(2)}, u32[]{:S(2)}) %all-to-all-start.1) | async-done | bytes 262176 | tf_op jit(solution)/shard_map/all_to_all | solution.py:18
  57.2 0.7 broadcast_in_dim.8
  57.9 4.8 %all-to-all-start.3 = ((f32[16,16,256]{2,1,0:T(8,128)}), f32[16,16,256]{2,1,0:T(8,128)S(1)}, u32[]{:S(2)}, u32[]{:S(2)}) async-start(f32[16,16,256]{2,1,0:T(8,128)} %broadcast_in_dim.8), calls=%async_computation.3 | async-start | bytes 524288 | tf_op jit(solution)/shard_map/all_to_all | solution.py:12
  62.7 8.8 %all-to-all-done.3 = f32[16,16,256]{2,1,0:T(8,128)S(1)} async-done(((f32[16,16,256]{2,1,0:T(8,128)}), f32[16,16,256]{2,1,0:T(8,128)S(1)}, u32[]{:S(2)}, u32[]{:S(2)}) %all-to-all-start.3) | async-done | bytes 262176 | tf_op jit(solution)/shard_map/all_to_all | solution.py:12
  71.7 0.4 convolution_multiply_fusion
  72.3 11.7 %cholesky.50 = f32[128,128]{1,0:T(8,128)S(1)} custom-call(f32[128,128]{1,0:T(8,128)S(1)} %cholesky.118), custom_call_target="Cholesky" | custom-call | tf_op jit(solution)/shard_map/jit(cholesky)/cholesky | solution.py:48
  84.1 9.8 %custom-call.16 = f32[1,128,128]{1,2,0:T(8,128)S(1)} custom-call(f32[1,128,128]{2,1,0:T(8,128)S(1)} %get-tuple-element.23), custom_call_target="InvertDiagBlocksLowerTriangular" | custom-call | tf_op jit(solution)/shard_map/jit(cholesky)/cholesky | solution.py:48
  93.9 0.2 constant_dynamic-update-slice_fusion.1
  94.1 0.3 convolution_subtract_fusion
  94.4 11.7 %cholesky.105 = f32[128,128]{1,0:T(8,128)S(1)} custom-call(f32[128,128]{1,0:T(8,128)S(1)} %convolution_subtract_fusion), custom_call_target="Cholesky" | custom-call | tf_op jit(solution)/shard_map/jit(cholesky)/cholesky | solution.py:48
  106.1 0.7 compare_reduce_fusion
  108.3 4.1 %while.1 = (s32[]{:T(128)}, f32[256,256]{1,0:T(8,128)S(1)}, s32[2,2]{1,0:T(2,128)S(1)}, f32[2,128,128]{2,1,0:T(8,128)S(1)}, s32[]{:T(128)}) while((s32[]{:T(128)}, f32[256,256]{1,0:T(8,128)S(1)}, s32[2,2]{1,0:T(2,128)S(1)}, f32[2,128,128]{2,1,0:T(8,128)S(1)}, s32[]{:T(128)}) %tuple.27), condition=%wide.while_cond, body=%wide.while_body.sunk | while | flops 2 | bytes 131189 | solution.py:49
  108.3 0.6 fusion.28
  108.9 1.4 bitcast_dynamic-update-slice_fusion.2
  110.4 0.6 fusion.28
  110.9 1.4 bitcast_dynamic-update-slice_fusion.2
  112.4 19.9 %custom-call.17 = f32[2,128,128]{1,2,0:T(8,128)S(1)} custom-call(f32[2,128,128]{2,1,0:T(8,128)S(1)} %get-tuple-element.9), custom_call_target="InvertDiagBlocksLowerTriangular" | custom-call | tf_op jit(solution)/shard_map/triangular_solve | solution.py:49
  132.4 0.2 convolution_subtract_fusion.2
  132.6 0.2 fusion.7
  132.8 0.2 fusion.6
  133.0 0.2 convolution_subtract_fusion.1
  133.2 0.2 fusion.4
  133.7 23.7 %all_to_all.26 = f32[256,1,256]{2,1,0:T(1,128)S(1)} all-to-all(f32[256,1,256]{2,1,0:T(1,128)S(1)} %broadcast_in_dim.9), channel_id=1, replica_groups=mesh['row'=16,'col'=16] {'row','col'}, dimensions={0} | all-to-all | bytes 524288 | tf_op jit(solution)/shard_map/all_to_all | solution.py:12
  157.3 0.3 reduce_sum.49
  157.6 0.6 fusion.10
  (23 shorter events, 0.9 us)
Async XLA Ops:
  0.6 71.0 %copy-start = (f32[32,256]{1,0:T(8,128)S(1)}, f32[32,256]{1,0:T(8,128)}, u32[]{:S(2)}) copy-start(f32[32,256]{1,0:T(8,128)} %param.5) | copy-start | bytes 98308
  26.0 17.0 %all-to-all-start.2 = ((f32[16,16,256]{2,1,0:T(8,128)}), f32[16,16,256]{2,1,0:T(8,128)S(1)}, u32[]{:S(2)}, u32[]{:S(2)}) async-start(f32[16,16,256]{2,1,0:T(8,128)} %fusion.13), calls=%async_computation.2 | async-start | bytes 524288 | tf_op jit(solution)/shard_map/all_to_all | solution.py:18
  43.0 14.2 %all-to-all-start.1 = ((f32[16,16,256]{2,1,0:T(8,128)}), f32[16,16,256]{2,1,0:T(8,128)S(1)}, u32[]{:S(2)}, u32[]{:S(2)}) async-start(f32[16,16,256]{2,1,0:T(8,128)} %bitcast.3), calls=%async_computation.1 | async-start | bytes 524288 | tf_op jit(solution)/shard_map/all_to_all | solution.py:18
  57.9 13.6 %all-to-all-start.3 = ((f32[16,16,256]{2,1,0:T(8,128)}), f32[16,16,256]{2,1,0:T(8,128)S(1)}, u32[]{:S(2)}, u32[]{:S(2)}) async-start(f32[16,16,256]{2,1,0:T(8,128)} %broadcast_in_dim.8), calls=%async_computation.3 | async-start | bytes 524288 | tf_op jit(solution)/shard_map/all_to_all | solution.py:12
  157.6 0.6 copy-start.1

commit v2 on v0

v2 whole, which is shorter than its diff:
```python
import functools

import jax
import jax.numpy as jnp
from jax import lax
from jax.experimental import pallas as pl
from jax.experimental.pallas import tpu as pltpu
from jax.sharding import PartitionSpec as P

eps = 1e-06
high = lax.Precision.HIGHEST
f32 = jnp.float32
bf16 = jnp.bfloat16
limit = 16 * 1024 * 1024
pivots = 16
lanes = 128
frames = 4
both = ("row", "col")
nt = (((1,), (1,)), ((), ()))


def interleave(core, mine, other):
    first = core == 0
    return jnp.concatenate(
        [jnp.where(first, mine, other), jnp.where(first, other, mine)], axis=1
    )


def gram_kernel(core_ref, mine_ref, other_ref, block_ref, part_ref):
    mine = mine_ref[...]
    count, width, cols_j = mine.shape
    block = interleave(core_ref[0], mine, other_ref[...]).reshape(2 * count * width, cols_j)
    block_ref[...] = block
    part = lax.dot_general(
        mine.reshape(count * width, cols_j), block, nt, precision=high, preferred_element_type=f32
    )
    part_ref[...] = part.reshape(part_ref.shape)


def partial_gram(core, mine, other, peers):
    count, width, cols_j = mine.shape
    ranks = 2 * count * width
    return pl.pallas_call(
        gram_kernel,
        out_shape=(
            jax.ShapeDtypeStruct((ranks, cols_j), f32),
            jax.ShapeDtypeStruct((peers, ranks // 2 // peers, ranks), f32),
        ),
        in_specs=[pl.BlockSpec(memory_space=pltpu.SMEM)]
        + [pl.BlockSpec(memory_space=pltpu.VMEM)] * 2,
        out_specs=[pl.BlockSpec(memory_space=pltpu.VMEM)] * 2,
        compiler_params=pltpu.CompilerParams(vmem_limit_bytes=limit),
        name="gram_part",
    )(core, mine, other)


def halves(value):
    top = value.astype(bf16)
    return top, (value - top.astype(f32)).astype(bf16)


def mttkrp_kernel(slab_ref, block_ref, c_ref, out_ref, split_ref):
    step = pl.program_id(0)

    @pl.when(step == 0)
    def _():
        top, low = halves(block_ref[...])
        split_ref[...] = jnp.concatenate([top, low, top], axis=1)
        out_ref[...] = jnp.zeros_like(out_ref)

    weights = split_ref[...]
    total = out_ref[...]
    for k in range(slab_ref.shape[0]):
        top, low = halves(slab_ref[k])
        product = lax.dot_general(
            jnp.concatenate([top, top, low], axis=1), weights, nt, preferred_element_type=f32
        )
        total += product * c_ref[k : k + 1]
    out_ref[...] = total


def mttkrp(slab, block, factor_c):
    depth, rows_i, cols_j = slab.shape
    ranks = block.shape[0]
    return pl.pallas_call(
        mttkrp_kernel,
        grid=(depth // frames,),
        out_shape=jax.ShapeDtypeStruct((rows_i, ranks), f32),
        in_specs=[
            pl.BlockSpec((frames, rows_i, cols_j), lambda s: (s, 0, 0)),
            pl.BlockSpec((ranks, cols_j), lambda s: (0, 0)),
            pl.BlockSpec((None, frames, ranks), lambda s: (s, 0, 0)),
        ],
        out_specs=pl.BlockSpec((rows_i, ranks), lambda s: (0, 0)),
        scratch_shapes=[pltpu.VMEM((ranks, 3 * cols_j), bf16)],
        compiler_params=pltpu.CompilerParams(vmem_limit_bytes=limit),
        cost_estimate=pl.CostEstimate(
            flops=6 * depth * rows_i * cols_j * ranks,
            bytes_accessed=4 * depth * rows_i * cols_j,
            transcendentals=0,
        ),
        name="mttkrp",
    )(slab, block, factor_c.reshape(depth // frames, frames, ranks))


def pack_kernel(parts_ref, terms_ref, out_ref):
    rows = parts_ref.shape[1]
    total = jnp.sum(parts_ref[...], axis=0)
    out_ref[:, :rows] = jnp.broadcast_to(total[None], parts_ref.shape)
    out_ref[:, rows:] = terms_ref[...].reshape(out_ref[:, rows:].shape)


def pack(parts, terms):
    peers, rows, ranks = parts.shape
    return pl.pallas_call(
        pack_kernel,
        out_shape=jax.ShapeDtypeStruct((peers, rows + terms.shape[0] // peers, ranks), f32),
        compiler_params=pltpu.CompilerParams(vmem_limit_bytes=limit),
        name="pack",
    )(parts, terms)


def invert(gram_ref):
    size = gram_ref.shape[0]

    def step(_, carry):
        head = gram_ref[:pivots]
        row = lax.broadcasted_iota(jnp.int32, (pivots, lanes), 0)
        lane = lax.broadcasted_iota(jnp.int32, (pivots, lanes), 1)
        cols = [jnp.broadcast_to(head[:, q : q + 1], (pivots, lanes)) for q in range(pivots)]
        turned = pltpu.roll(head, size - pivots, axis=1)
        left, right = turned[:, :lanes], turned[:, lanes:]
        for q in range(pivots):
            here = row == q
            col = cols[q]
            inverse = jnp.broadcast_to(1.0 / col[q : q + 1], col.shape)
            factor = jnp.where(here, -inverse, col * inverse)
            for p in range(q + 1, pivots):
                top = jnp.broadcast_to(cols[p][q : q + 1], col.shape)
                cols[p] = jnp.where(here, 0.0, cols[p]) - factor * top
            own = lane == lanes - pivots + q
            top = jnp.broadcast_to(left[q : q + 1], left.shape)
            left = jnp.where(here, 0.0, left) - factor * top
            top = jnp.where(own, 1.0, jnp.broadcast_to(right[q : q + 1], right.shape))
            right = jnp.where(here | own, 0.0, right) - factor * top
        done = jnp.concatenate([left, right], axis=1)
        rest = gram_ref[pivots:]
        lane = lax.broadcasted_iota(jnp.int32, rest.shape, 1)
        base = pltpu.roll(jnp.where(lane < pivots, 0.0, rest), size - pivots, axis=1)
        update = jnp.dot(rest[:, :pivots], done, precision=high, preferred_element_type=f32)
        gram_ref[: size - pivots] = base - update
        gram_ref[size - pivots :] = done
        return carry

    lax.fori_loop(0, size // pivots, step, 0)


def solve_kernel(core_ref, packed_ref, other_ref, c_ref, solved_ref, squares_ref, gram_ref):
    other = other_ref[...]
    peers, rows, ranks = other.shape
    shape = (peers // 2, 2 * rows, ranks)
    gram_b = interleave(
        core_ref[0], packed_ref[:, :rows].reshape(shape), other.reshape(shape)
    ).reshape(ranks, ranks)
    c = c_ref[...]
    gram_c = lax.dot_general(
        c, c, (((0,), (0,)), ((), ())), precision=high, preferred_element_type=f32
    )
    gram_ref[...] = gram_b * gram_c
    invert(gram_ref)
    mine = jnp.sum(packed_ref[:, rows:], axis=0)
    solved = jnp.dot(mine, gram_ref[...], precision=high, preferred_element_type=f32)
    solved_ref[...] = solved
    squares_ref[...] = jnp.sum(solved * solved, axis=0, keepdims=True)


def solve(core, packed, other, factor_c):
    peers, rows, ranks = other.shape
    return pl.pallas_call(
        solve_kernel,
        out_shape=(
            jax.ShapeDtypeStruct((packed.shape[1] - rows, ranks), f32),
            jax.ShapeDtypeStruct((1, ranks), f32),
        ),
        in_specs=[pl.BlockSpec(memory_space=pltpu.SMEM)]
        + [pl.BlockSpec(memory_space=pltpu.VMEM)] * 3,
        scratch_shapes=[pltpu.VMEM((ranks, ranks), f32)],
        compiler_params=pltpu.CompilerParams(vmem_limit_bytes=limit),
        name="solve",
    )(core, packed, other, factor_c)


def local(tensor, factor_b, factor_c):
    depth, rows_i, cols_j = tensor.shape
    n_row, n_col = lax.axis_size("row"), lax.axis_size("col")
    core = (lax.axis_index("row") % 2).astype(jnp.int32)[None]
    chips = n_row // 2
    same_core = [[2 * chip + core for chip in range(chips)] for core in range(2)]
    swap = [(i, i ^ 1) for i in range(n_row)]
    width = factor_b.shape[1]

    copies = jnp.broadcast_to(factor_b.T[None], (chips, width, cols_j))
    mine = lax.all_to_all(copies, "row", 0, 0, axis_index_groups=same_core)
    other = lax.ppermute(mine, "row", swap)
    block, parts = partial_gram(core, mine, other, n_col)
    parts = lax.all_to_all(parts, "col", 0, 0)
    terms = mttkrp(tensor, block, factor_c)
    packed = lax.all_to_all(pack(parts, terms), "col", 0, 0)
    other = lax.ppermute(packed[:, : parts.shape[1]], "row", swap)
    solved, squares = solve(core, packed, other, factor_c)
    squares = squares + lax.ppermute(squares, "row", swap)
    same_core = [
        [(2 * chip + core) * n_col + c for chip in range(chips) for c in range(n_col)]
        for core in range(2)
    ]
    copies = jnp.broadcast_to(squares[None], (chips * n_col,) + squares.shape)
    squares = lax.all_to_all(copies, both, 0, 0, axis_index_groups=same_core)
    squares = jnp.sum(squares[:, 0], axis=0)
    col_scale = jnp.sqrt(squares / (rows_i * n_row) + eps)
    return (solved / col_scale, col_scale)


def solution(mesh):
    return jax.shard_map(
        local,
        mesh=mesh,
        in_specs=(P(None, "row", "col"), P("col", "row"), P()),
        out_specs=(P(both, None), P()),
        check_vma=False,
    )
```

time: 357 us -> 93.1 us (0.26)
  waiting for transfers between devices: 146 us -> 2.02 us
  blocking collectives: 121 us -> 56.7 us
  other arithmetic: 54.7 us -> 0.78 us
  Pallas kernels: 0 us -> 16.6 us
  matrix products: 15.5 us -> 0 us
  between operations: 15.4 us -> 0.71 us
  starting transfers between devices: 0.04 us -> 10.8 us
    psum x1 -> x0, waiting for transfers between devices: 146 us -> none  [sum_gram(): return lax.psum(partial_gram, 'col')]
    psum x1 -> x0, blocking collectives: 85.5 us -> none  [local(): squares = lax.psum(jnp.sum(solved * solved, axis=0), ('row', 'col'))]
    all_to_all x0 -> x3, blocking collectives: none -> 56.7 us  [the longest x1 20.8 us: local(): mine = lax.all_to_all(copies, 'row', 0, 0, axis_index_groups=same_core)]
    another operation x9 -> x0, other arithmetic: 53.9 us -> none  [the longest x6 34 us: local(): lower = jnp.linalg.cholesky(gram)]
    all_gather x1 -> x0, blocking collectives: 35.7 us -> none  [local(): block_b = lax.all_gather(factor_b, 'row', axis=1, tiled=True)]
    pallas_call x0 -> x4, Pallas kernels: none -> 16.6 us  [the longest x1 10.5 us: solve(): pl.pallas_call(solve_kernel, out_shape=(jax.ShapeDtypeStruct((packed.shap...]
    dot_general x3 -> x0, matrix products: 12.5 us -> none  [the longest x1 10.1 us: contract_rows(): jnp.dot(slab.reshape(depth * count, cols_j), block_b, precision=high, pre...]
    all_to_all x0 -> x1, starting transfers between devices: none -> 5.49 us  [local(): parts = lax.all_to_all(parts, 'col', 0, 0)]
  transfers between devices with their start and end apart: 1 -> 4, of which waited for: 1 -> 3; matrix products, arithmetic and copies ran while one was open for 0% -> 1% of each run, Pallas kernels for 0% -> 5%
where the time goes in v2:
time: 93.1 us; the launch traced here: 92.7 us
  blocking collectives  56.7 us (61%)
  Pallas kernels  16.6 us (18%)
  starting transfers between devices  10.8 us (12%)
  local copies, waits for them, and re-layouts  4.97 us (5%)
  waiting for transfers between devices  2.02 us (2%)
    all_to_all x1, blocking collectives, local(): mine = lax.all_to_all(copies, 'row', 0, 0, axis_index_groups=same_core)  20.8 us
    all_to_all x1, blocking collectives, local(): packed = lax.all_to_all(pack(parts, terms), 'col', 0, 0)  18.2 us
    all_to_all x1, blocking collectives, local(): squares = lax.all_to_all(copies, both, 0, 0, axis_index_groups=same_core)  17.8 us
    pallas_call x1, Pallas kernels, solve(): pl.pallas_call(solve_kernel, out_shape=(jax.ShapeDtypeStruct((packed.shap...  10.5 us
    all_to_all x1, starting transfers between devices, local(): parts = lax.all_to_all(parts, 'col', 0, 0)  5.49 us
    pallas_call x1, Pallas kernels, mttkrp(): pl.pallas_call(mttkrp_kernel, grid=(depth // frames,), out_shape=jax.Shap...  5.03 us
    unnamed x6, local copies, waits for them, and re-layouts  3.39 us
    ppermute x1, starting transfers between devices, local(): other = lax.ppermute(packed[:, :parts.shape[1]], 'row', swap)  2.8 us
  transfers between devices with their start and end apart: 4, of which 3 were waited for; matrix products, arithmetic and copies ran while one was open for 1% of the time, Pallas kernels for 5%

profile of v2, /device:TPU:1, one launch (start us, length us, event | category | flops | bytes accessed | tf_op | source)
XLA Modules:
  0.0 92.7 jit_solution(3597216050707305095)
XLA Ops:
  0.6 0.0 copy-start
  0.6 0.7 broadcast_in_dim.9
  1.4 20.8 %all_to_all.20.mine_ref = f32[8,16,256]{2,1,0:T(8,128)S(1)} all-to-all(f32[8,16,256]{2,1,0:T(8,128)S(1)} %broadcast_in_dim.9), channel_id=1, replica_groups={{0,32,64,96,128,160,192,224},{16,48,80,112,144,176,208,240},{1,33,65,97..., dimensions={0} | all-to-all | bytes 262144 | tf_op jit(solution)/shard_map/all_to_all | solution.py:203
  22.2 2.1 %collective-permute-start = (f32[8,16,256]{2,1,0:T(8,128)S(1)}, f32[8,16,256]{2,1,0:T(8,128)S(1)}, u32[]{:S(2)}, u32[]{:S(2)}) collective-permute-start(f32[8,16,256]{2,1,0:T(8,128)S(1)} %all_to_all.20.mine_ref), channel_id=1, source_target_pairs={{0,16},{16,0},{32,48},{48,32},{64,80},{80,64},{96,112},{112,96},{1... | collective-permute-start | bytes 393224 | tf_op jit(solution)/shard_map/ppermute | solution.py:204
  24.3 0.8 reshape.16.c_ref
  25.0 0.2 collective-permute-done.other_ref
  25.3 1.1 %gram_part.1 = (f32[256,256]{1,0:T(8,128)S(1)}, f32[16,8,256]{2,1,0:T(8,128)}) custom-call(s32[1]{0:T(128)} %bitcast.core_ref, f32[8,16,256]{2,1,0:T(8,128)S(1)} %all_to_all.20.mine_ref, f32[8,16,256]{2,1,0:T(8,128)S(1)} %collective-permute-done.other_ref), custom_call_target="tpu_custom_call" | custom-call | tf_op jit(solution)/shard_map/gram_part/pallas_call | solution.py:43
  26.3 5.5 %all-to-all-start.1 = ((f32[16,8,256]{2,1,0:T(8,128)}), f32[16,8,256]{2,1,0:T(8,128)S(1)}, u32[]{:S(2)}, u32[]{:S(2)}) async-start(f32[16,8,256]{2,1,0:T(8,128)} %get-tuple-element.6), calls=%async_computation.1 | async-start | bytes 262144 | tf_op jit(solution)/shard_map/all_to_all | solution.py:206
  31.8 0.0 copy-start.1
  31.8 3.4 %copy-done.1 = f32[32,256,256]{2,1,0:T(8,128)S(1)} copy-done((f32[32,256,256]{2,1,0:T(8,128)S(1)}, f32[32,256,256]{2,1,0:T(8,128)}, u32[]{:S(2)}) %copy-start.1) | copy-done | bytes 8388632
  35.2 5.0 %mttkrp.1.terms_ref = f32[256,256]{1,0:T(8,128)S(1)} custom-call(f32[32,256,256]{2,1,0:T(8,128)S(1)} %copy-done.1, f32[256,256]{1,0:T(8,128)S(1)} %get-tuple-element.7.block_ref, f32[8,4,256]{2,1,0:T(4,128)S(1)} %reshape.16.c_ref), custom_call_target="tpu_custom_call" | custom-call | flops 3221225472 | bytes 8388608 | tf_op jit(solution)/shard_map/mttkrp/pallas_call | solution.py:85
  40.2 0.0 all-to-all-done.1.parts_ref
  40.3 18.2 %all_to_all.21.packed_ref = f32[16,24,256]{2,1,0:T(8,128)S(1)} all-to-all(f32[16,24,256]{2,1,0:T(8,128)S(1)} %pack.1), channel_id=1, replica_groups=mesh['row'=16,'col'=16] {'col'}, dimensions={0} | all-to-all | bytes 786432 | tf_op jit(solution)/shard_map/all_to_all | solution.py:208
  58.5 2.8 %collective-permute-start.1 = (f32[16,8,256]{2,1,0:T(8,128)S(1)}, f32[16,8,256]{2,1,0:T(8,128)S(1)}, u32[]{:S(2)}, u32[]{:S(2)}) collective-permute-start(f32[16,8,256]{2,1,0:T(8,128)S(1)} %slice.4), channel_id=1, source_target_pairs={{0,16},{16,0},{32,48},{48,32},{64,80},{80,64},{96,112},{112,96},{1... | collective-permute-start | bytes 393224 | tf_op jit(solution)/shard_map/ppermute | solution.py:209
  61.3 1.0 %collective-permute-done.1.other_ref = f32[16,8,256]{2,1,0:T(8,128)S(1)} collective-permute-done((f32[16,8,256]{2,1,0:T(8,128)S(1)}, f32[16,8,256]{2,1,0:T(8,128)S(1)}, u32[]{:S(2)}, u32[]{:S(2)}) %collective-permute-start.1) | collective-permute-done | bytes 131104 | tf_op jit(solution)/shard_map/ppermute | solution.py:209
  62.3 0.0 copy-done
  62.3 10.5 %solve.1 = (f32[16,256]{1,0:T(8,128)S(1)}, f32[1,256]{1,0:T(1,128)S(1)}) custom-call(s32[1]{0:T(128)} %bitcast.core_ref, f32[16,24,256]{2,1,0:T(8,128)S(1)} %all_to_all.21.packed_ref, f32[16,8,256]{2,1,0:T(8,128)S(1)} %collective-permute-done.1.other_ref, f32[32,256]{1,0:T(8,128)S(1)} %copy-done), custom_call_target="tpu_custom_call" | custom-call | tf_op jit(solution)/shard_map/solve/pallas_call | solution.py:179
  72.8 0.4 collective-permute-start.2
  73.2 0.8 collective-permute-done.2
  74.1 0.1 broadcast_in_dim.21
  74.1 17.8 %all_to_all.22 = f32[128,1,256]{2,1,0:T(1,128)S(1)} all-to-all(f32[128,1,256]{2,1,0:T(1,128)S(1)} %broadcast_in_dim.21), channel_id=1, replica_groups={{0,1,2,3,4,5,6,7,8,9,10,11,12,13,14,15,32,33,34,35,36,37,38,39,40,41,42..., dimensions={0} | all-to-all | bytes 262144 | tf_op jit(solution)/shard_map/all_to_all | solution.py:217
  91.9 0.2 reduce_sum.9
  92.1 0.0 copy-start.2
  92.1 0.6 broadcast_divide_fusion
  92.7 0.0 copy-done.2
  (4 shorter events, 0.1 us)
Async XLA Ops:
  0.6 61.7 %copy-start = (f32[32,256]{1,0:T(8,128)S(1)}, f32[32,256]{1,0:T(8,128)}, u32[]{:S(2)}) copy-start(f32[32,256]{1,0:T(8,128)} %c_ref.1) | copy-start | bytes 98308
  22.2 3.1 %collective-permute-start = (f32[8,16,256]{2,1,0:T(8,128)S(1)}, f32[8,16,256]{2,1,0:T(8,128)S(1)}, u32[]{:S(2)}, u32[]{:S(2)}) collective-permute-start(f32[8,16,256]{2,1,0:T(8,128)S(1)} %all_to_all.20.mine_ref), channel_id=1, source_target_pairs={{0,16},{16,0},{32,48},{48,32},{64,80},{80,64},{96,112},{112,96},{1... | collective-permute-start | bytes 393224 | tf_op jit(solution)/shard_map/ppermute | solution.py:204
  26.3 13.9 %all-to-all-start.1 = ((f32[16,8,256]{2,1,0:T(8,128)}), f32[16,8,256]{2,1,0:T(8,128)S(1)}, u32[]{:S(2)}, u32[]{:S(2)}) async-start(f32[16,8,256]{2,1,0:T(8,128)} %get-tuple-element.6), calls=%async_computation.1 | async-start | bytes 262144 | tf_op jit(solution)/shard_map/all_to_all | solution.py:206
  31.8 3.4 %copy-start.1 = (f32[32,256,256]{2,1,0:T(8,128)S(1)}, f32[32,256,256]{2,1,0:T(8,128)}, u32[]{:S(2)}) copy-start(f32[32,256,256]{2,1,0:T(8,128)} %slab_ref.1) | copy-start | bytes 25165828
  58.5 3.8 %collective-permute-start.1 = (f32[16,8,256]{2,1,0:T(8,128)S(1)}, f32[16,8,256]{2,1,0:T(8,128)S(1)}, u32[]{:S(2)}, u32[]{:S(2)}) collective-permute-start(f32[16,8,256]{2,1,0:T(8,128)S(1)} %slice.4), channel_id=1, source_target_pairs={{0,16},{16,0},{32,48},{48,32},{64,80},{80,64},{96,112},{112,96},{1... | collective-permute-start | bytes 393224 | tf_op jit(solution)/shard_map/ppermute | solution.py:209
  72.8 1.3 %collective-permute-start.2 = (f32[1,256]{1,0:T(1,128)S(1)}, f32[1,256]{1,0:T(1,128)S(1)}, u32[]{:S(2)}, u32[]{:S(2)}) collective-permute-start(f32[1,256]{1,0:T(1,128)S(1)} %get-tuple-element.9), channel_id=1, source_target_pairs={{0,16},{16,0},{32,48},{48,32},{64,80},{80,64},{96,112},{112,96},{1... | collective-permute-start | bytes 3080 | tf_op jit(solution)/shard_map/ppermute | solution.py:211
  92.1 0.6 copy-start.2

commit v3 on v2

v3 whole, which is shorter than its diff:
```python
import functools

import jax
import jax.numpy as jnp
from jax import lax
from jax.experimental import pallas as pl
from jax.experimental.pallas import tpu as pltpu
from jax.sharding import PartitionSpec as P

eps = 1e-06
high = lax.Precision.HIGHEST
f32 = jnp.float32
bf16 = jnp.bfloat16
limit = 16 * 1024 * 1024
wide = 52 * 1024 * 1024
pivots = 16
lanes = 128
frames = (4, 12, 16)
both = ("row", "col")
nt = (((1,), (1,)), ((), ()))


def interleave(core, mine, other):
    first = core == 0
    return jnp.concatenate(
        [jnp.where(first, mine, other), jnp.where(first, other, mine)], axis=1
    )


def gram_kernel(core_ref, mine_ref, other_ref, block_ref, part_ref):
    mine = mine_ref[...]
    count, width, cols_j = mine.shape
    block = interleave(core_ref[0], mine, other_ref[...]).reshape(2 * count * width, cols_j)
    block_ref[...] = block
    part = lax.dot_general(
        mine.reshape(count * width, cols_j), block, nt, precision=high, preferred_element_type=f32
    )
    part_ref[...] = part.reshape(part_ref.shape)


def partial_gram(core, mine, other, peers):
    count, width, cols_j = mine.shape
    ranks = 2 * count * width
    return pl.pallas_call(
        gram_kernel,
        out_shape=(
            jax.ShapeDtypeStruct((ranks, cols_j), f32),
            jax.ShapeDtypeStruct((peers, ranks // 2 // peers, ranks), f32),
        ),
        in_specs=[pl.BlockSpec(memory_space=pltpu.SMEM)]
        + [pl.BlockSpec(memory_space=pltpu.VMEM)] * 2,
        out_specs=[pl.BlockSpec(memory_space=pltpu.VMEM)] * 2,
        compiler_params=pltpu.CompilerParams(vmem_limit_bytes=limit),
        name="gram_part",
    )(core, mine, other)


def halves(value):
    top = value.astype(bf16)
    return top, (value - top.astype(f32)).astype(bf16)


def mttkrp_kernel(slab_hbm, block_ref, c_hbm, out_ref, gram_c_ref, slab_ref, c_ref, arrived):
    pieces = []
    first = 0
    for part, count in enumerate(frames):
        here = pl.ds(first, count)
        copy = pltpu.make_async_copy(slab_hbm.at[here], slab_ref.at[here], arrived.at[part])
        pieces.append((copy, range(first, first + count)))
        first += count
    c_copy = pltpu.make_async_copy(c_hbm, c_ref, arrived.at[len(frames)])
    c_copy.start()
    for copy, _ in pieces:
        copy.start()
    c_copy.wait()
    c = c_ref[...]
    gram_c_ref[...] = lax.dot_general(
        c, c, (((0,), (0,)), ((), ())), precision=high, preferred_element_type=f32
    )
    top, low = halves(block_ref[...])
    weights = jnp.concatenate([top, low, top], axis=1)
    total = jnp.zeros(out_ref.shape, f32)
    for copy, here in pieces:
        copy.wait()
        for k in here:
            top, low = halves(slab_ref[k])
            product = lax.dot_general(
                jnp.concatenate([top, top, low], axis=1), weights, nt, preferred_element_type=f32
            )
            total += product * c[k : k + 1]
    out_ref[...] = total


def mttkrp(slab, block, factor_c):
    depth, rows_i, cols_j = slab.shape
    ranks = block.shape[0]
    return pl.pallas_call(
        mttkrp_kernel,
        out_shape=(
            jax.ShapeDtypeStruct((rows_i, ranks), f32),
            jax.ShapeDtypeStruct((ranks, ranks), f32),
        ),
        in_specs=[
            pl.BlockSpec(memory_space=pl.ANY),
            pl.BlockSpec(memory_space=pltpu.VMEM),
            pl.BlockSpec(memory_space=pl.ANY),
        ],
        scratch_shapes=[
            pltpu.VMEM(slab.shape, f32),
            pltpu.VMEM(factor_c.shape, f32),
            pltpu.SemaphoreType.DMA((len(frames) + 1,)),
        ],
        compiler_params=pltpu.CompilerParams(vmem_limit_bytes=wide),
        cost_estimate=pl.CostEstimate(
            flops=6 * depth * rows_i * cols_j * ranks,
            bytes_accessed=4 * depth * rows_i * cols_j,
            transcendentals=0,
        ),
        name="mttkrp",
    )(slab, block, factor_c)


def pack_kernel(parts_ref, terms_ref, out_ref):
    rows = parts_ref.shape[1]
    total = jnp.sum(parts_ref[...], axis=0)
    out_ref[:, :rows] = jnp.broadcast_to(total[None], parts_ref.shape)
    out_ref[:, rows:] = terms_ref[...].reshape(out_ref[:, rows:].shape)


def pack(parts, terms):
    peers, rows, ranks = parts.shape
    return pl.pallas_call(
        pack_kernel,
        out_shape=jax.ShapeDtypeStruct((peers, rows + terms.shape[0] // peers, ranks), f32),
        compiler_params=pltpu.CompilerParams(vmem_limit_bytes=limit),
        name="pack",
    )(parts, terms)


def split(value):
    top = value.astype(bf16)
    rest = value - top.astype(f32)
    middle = rest.astype(bf16)
    return top, middle, (rest - middle.astype(f32)).astype(bf16)


def left_parts(value):
    top, middle, low = split(value)
    return jnp.concatenate([top, top, middle, top, middle, low], axis=1)


def right_parts(value):
    top, middle, low = split(value)
    return jnp.concatenate([top, middle, top, low, middle, top], axis=0)


def eliminate(tiles, tile, offset):
    shape = tiles[0].shape
    row = lax.broadcasted_iota(jnp.int32, shape, 0)
    lane = lax.broadcasted_iota(jnp.int32, shape, 1) - offset
    cols = [
        jnp.broadcast_to(tiles[tile][:, offset + q : offset + q + 1], shape) for q in range(pivots)
    ]
    unit = jnp.where(lane == row, 1.0, 0.0)
    tiles = list(tiles)
    tiles[tile] = jnp.where((lane >= 0) & (lane < pivots), unit, tiles[tile])
    scale = jnp.ones(shape, f32)
    for q in range(pivots):
        here = row == q
        inverse = jnp.broadcast_to(1.0 / cols[q][q : q + 1], shape)
        factor = jnp.where(here, 0.0, cols[q] * inverse)
        scale = jnp.where(here, inverse, scale)
        for p in range(q + 1, pivots):
            cols[p] = cols[p] - factor * jnp.broadcast_to(cols[p][q : q + 1], shape)
        tiles = [part - factor * jnp.broadcast_to(part[q : q + 1], shape) for part in tiles]
    return [part * scale for part in tiles]


def invert(gram_ref):
    size = gram_ref.shape[0]
    starts = range(0, size, lanes)
    for k0 in range(0, size, pivots):
        k1 = k0 + pivots
        k2 = min(k1 + pivots, size)
        tiles = [gram_ref[k0:k2, t : t + lanes] for t in starts]
        tiles = eliminate(tiles, k0 // lanes, k0 % lanes)
        done = jnp.concatenate([part[:pivots] for part in tiles], axis=1)
        right = right_parts(done)
        if k2 > k1:
            for part, t in zip(tiles, starts):
                gram_ref[k1:k2, t : t + lanes] = part[pivots:]

        def update(first, last):
            if first < last:
                rows = gram_ref[first:last]
                lane = lax.broadcasted_iota(jnp.int32, rows.shape, 1)
                base = jnp.where((lane >= k0) & (lane < k1), 0.0, rows)
                gram_ref[first:last] = base - jnp.dot(
                    left_parts(rows[:, k0:k1]), right, preferred_element_type=f32
                )

        update(k2, min(k2 + pivots, size))
        update(k2 + pivots, size)
        update(0, k0)
        gram_ref[k0:k1] = done


def solve_kernel(core_ref, packed_ref, other_ref, gram_c_ref, solved_ref, squares_ref, gram_ref):
    other = other_ref[...]
    peers, rows, ranks = other.shape
    shape = (peers // 2, 2 * rows, ranks)
    gram_b = interleave(
        core_ref[0], packed_ref[:, :rows].reshape(shape), other.reshape(shape)
    ).reshape(ranks, ranks)
    gram_ref[...] = gram_b * gram_c_ref[...]
    invert(gram_ref)
    mine = jnp.sum(packed_ref[:, rows:], axis=0)
    solved = jnp.dot(mine, gram_ref[...], precision=high, preferred_element_type=f32)
    solved_ref[...] = solved
    squares_ref[...] = jnp.sum(solved * solved, axis=0, keepdims=True)


def solve(core, packed, other, gram_c):
    peers, rows, ranks = other.shape
    return pl.pallas_call(
        solve_kernel,
        out_shape=(
            jax.ShapeDtypeStruct((packed.shape[1] - rows, ranks), f32),
            jax.ShapeDtypeStruct((1, ranks), f32),
        ),
        in_specs=[pl.BlockSpec(memory_space=pltpu.SMEM)]
        + [pl.BlockSpec(memory_space=pltpu.VMEM)] * 3,
        scratch_shapes=[pltpu.VMEM((ranks, ranks), f32)],
        compiler_params=pltpu.CompilerParams(vmem_limit_bytes=limit),
        name="solve",
    )(core, packed, other, gram_c)


def finish_kernel(count, squares_ref, solved_ref, factor_ref, scale_ref):
    squares = jnp.sum(squares_ref[...], axis=0)
    scale = jnp.sqrt(squares / count + eps)
    scale_ref[...] = scale
    factor_ref[...] = solved_ref[...] / scale


def finish(squares, solved, count):
    return pl.pallas_call(
        functools.partial(finish_kernel, count),
        out_shape=(
            jax.ShapeDtypeStruct(solved.shape, f32),
            jax.ShapeDtypeStruct((1, solved.shape[1]), f32),
        ),
        compiler_params=pltpu.CompilerParams(vmem_limit_bytes=limit),
        name="finish",
    )(squares, solved)


def local(tensor, factor_b, factor_c):
    depth, rows_i, cols_j = tensor.shape
    n_row, n_col = lax.axis_size("row"), lax.axis_size("col")
    core = (lax.axis_index("row") % 2).astype(jnp.int32)[None]
    chips = n_row // 2
    same_core = [[2 * chip + core for chip in range(chips)] for core in range(2)]
    swap = [(i, i ^ 1) for i in range(n_row)]
    width = factor_b.shape[1]

    copies = jnp.broadcast_to(factor_b.T[None], (chips, width, cols_j))
    mine = lax.all_to_all(copies, "row", 0, 0, axis_index_groups=same_core)
    other = lax.ppermute(mine, "row", swap)
    block, parts = partial_gram(core, mine, other, n_col)
    parts = lax.all_to_all(parts, "col", 0, 0)
    terms, gram_c = mttkrp(tensor, block, factor_c)
    packed = lax.all_to_all(pack(parts, terms), "col", 0, 0)
    other = lax.ppermute(packed[:, : parts.shape[1]], "row", swap)
    solved, squares = solve(core, packed, other, gram_c)
    squares = squares + lax.ppermute(squares, "row", swap)
    same_core = [
        [(2 * chip + core) * n_col + c for chip in range(chips) for c in range(n_col)]
        for core in range(2)
    ]
    copies = jnp.broadcast_to(squares[None], (chips * n_col,) + squares.shape)
    squares = lax.all_to_all(copies, both, 0, 0, axis_index_groups=same_core)
    factor_a, col_scale = finish(squares, solved, rows_i * n_row)
    return (factor_a, col_scale[0])


def solution(mesh):
    return jax.shard_map(
        local,
        mesh=mesh,
        in_specs=(P(None, "row", "col"), P("col", "row"), P()),
        out_specs=(P(both, None), P()),
        check_vma=False,
    )
```

time: 93.1 us -> 87.1 us (0.936)
  local copies, waits for them, and re-layouts: 4.97 us -> 1.56 us
  Pallas kernels: 16.6 us -> 14.1 us
  waiting for transfers between devices: 2.02 us -> 4.24 us
  blocking collectives: 56.7 us -> 55.3 us
    pallas_call x1, Pallas kernels: 10.5 us -> 6.67 us  [solve(): pl.pallas_call(solve_kernel, out_shape=(jax.ShapeDtypeStruct((packed.shap...]
    unnamed x6 -> x2, local copies, waits for them, and re-layouts: 3.39 us -> 0.75 us
    all_to_all x1, waiting for transfers between devices: 0.01 us -> 1.45 us  [local(): parts = lax.all_to_all(parts, 'col', 0, 0)]
    all_to_all x1, blocking collectives: 18.2 us -> 16.7 us  [local(): packed = lax.all_to_all(pack(parts, terms), 'col', 0, 0)]
    pallas_call x1 -> x2, Pallas kernels: 5.03 us -> 6.33 us  [the longest x1 5.56 us: mttkrp(): pl.pallas_call(mttkrp_kernel, out_shape=(jax.ShapeDtypeStruct((rows_i, ra...]
  transfers between devices with their start and end apart: 4 -> 4, of which waited for: 3 -> 4; matrix products, arithmetic and copies ran while one was open for 1% -> 0% of each run, Pallas kernels for 5% -> 6%
where the time goes in v3:
time: 87.1 us; the launch traced here: 86.7 us
  blocking collectives  55.3 us (63%)
  Pallas kernels  14.1 us (16%)
  starting transfers between devices  10.9 us (13%)
  waiting for transfers between devices  4.24 us (5%)
  local copies, waits for them, and re-layouts  1.56 us (2%)
    all_to_all x1, blocking collectives, local(): mine = lax.all_to_all(copies, 'row', 0, 0, axis_index_groups=same_core)  20.8 us
    all_to_all x1, blocking collectives, local(): squares = lax.all_to_all(copies, both, 0, 0, axis_index_groups=same_core)  17.7 us
    all_to_all x1, blocking collectives, local(): packed = lax.all_to_all(pack(parts, terms), 'col', 0, 0)  16.7 us
    pallas_call x1, Pallas kernels, solve(): pl.pallas_call(solve_kernel, out_shape=(jax.ShapeDtypeStruct((packed.shap...  6.67 us
    pallas_call x1, Pallas kernels, mttkrp(): pl.pallas_call(mttkrp_kernel, out_shape=(jax.ShapeDtypeStruct((rows_i, ra...  5.56 us
    all_to_all x1, starting transfers between devices, local(): parts = lax.all_to_all(parts, 'col', 0, 0)  5.49 us
    ppermute x1, starting transfers between devices, local(): other = lax.ppermute(packed[:, :parts.shape[1]], 'row', swap)  2.81 us
    ppermute x1, starting transfers between devices, local(): other = lax.ppermute(mine, 'row', swap)  2.1 us
  transfers between devices with their start and end apart: 4, of which 4 were waited for; matrix products, arithmetic and copies ran while one was open for 0% of the time, Pallas kernels for 6%

profile of v3, /device:TPU:1, one launch (start us, length us, event | category | flops | bytes accessed | tf_op | source)
XLA Modules:
  0.0 86.7 jit_solution(6186279326427872953)
XLA Ops:
  0.6 0.7 broadcast_in_dim.18
  1.4 20.8 %all_to_all.20.mine_ref = f32[8,16,256]{2,1,0:T(8,128)S(1)} all-to-all(f32[8,16,256]{2,1,0:T(8,128)S(1)} %broadcast_in_dim.18), channel_id=1, replica_groups={{0,32,64,96,128,160,192,224},{16,48,80,112,144,176,208,240},{1,33,65,97..., dimensions={0} | all-to-all | bytes 262144 | tf_op jit(solution)/shard_map/all_to_all | solution.py:268
  22.1 2.1 %collective-permute-start = (f32[8,16,256]{2,1,0:T(8,128)S(1)}, f32[8,16,256]{2,1,0:T(8,128)S(1)}, u32[]{:S(2)}, u32[]{:S(2)}) collective-permute-start(f32[8,16,256]{2,1,0:T(8,128)S(1)} %all_to_all.20.mine_ref), channel_id=1, source_target_pairs={{0,16},{16,0},{32,48},{48,32},{64,80},{80,64},{96,112},{112,96},{1... | collective-permute-start | bytes 393224 | tf_op jit(solution)/shard_map/ppermute | solution.py:269
  24.2 1.0 %collective-permute-done.other_ref = f32[8,16,256]{2,1,0:T(8,128)S(1)} collective-permute-done((f32[8,16,256]{2,1,0:T(8,128)S(1)}, f32[8,16,256]{2,1,0:T(8,128)S(1)}, u32[]{:S(2)}, u32[]{:S(2)}) %collective-permute-start) | collective-permute-done | bytes 131104 | tf_op jit(solution)/shard_map/ppermute | solution.py:269
  25.2 1.1 %gram_part.1 = (f32[256,256]{1,0:T(8,128)S(1)}, f32[16,8,256]{2,1,0:T(8,128)}) custom-call(s32[1]{0:T(128)} %bitcast.core_ref, f32[8,16,256]{2,1,0:T(8,128)S(1)} %all_to_all.20.mine_ref, f32[8,16,256]{2,1,0:T(8,128)S(1)} %collective-permute-done.other_ref), custom_call_target="tpu_custom_call" | custom-call | tf_op jit(solution)/shard_map/gram_part/pallas_call | solution.py:44
  26.3 5.5 %all-to-all-start.1 = ((f32[16,8,256]{2,1,0:T(8,128)}), f32[16,8,256]{2,1,0:T(8,128)S(1)}, u32[]{:S(2)}, u32[]{:S(2)}) async-start(f32[16,8,256]{2,1,0:T(8,128)} %get-tuple-element.10), calls=%async_computation.1 | async-start | bytes 262144 | tf_op jit(solution)/shard_map/all_to_all | solution.py:271
  31.8 0.0 copy-start
  31.8 0.7 copy-done
  32.6 5.6 %mttkrp.1 = (f32[256,256]{1,0:T(8,128)S(1)}, f32[256,256]{1,0:T(8,128)S(1)}) custom-call(f32[32,256,256]{2,1,0:T(8,128)} %slab_hbm.1, f32[256,256]{1,0:T(8,128)S(1)} %get-tuple-element.11.block_ref, f32[32,256]{1,0:T(8,128)S(1)} %copy-done), custom_call_target="tpu_custom_call" | custom-call | flops 3221225472 | bytes 8388608 | tf_op jit(solution)/shard_map/mttkrp/pallas_call | solution.py:97
  38.1 1.5 %all-to-all-done.1.parts_ref = f32[16,8,256]{2,1,0:T(8,128)S(1)} async-done(((f32[16,8,256]{2,1,0:T(8,128)}), f32[16,8,256]{2,1,0:T(8,128)S(1)}, u32[]{:S(2)}, u32[]{:S(2)}) %all-to-all-start.1) | async-done | bytes 131104 | tf_op jit(solution)/shard_map/all_to_all | solution.py:271
  39.6 16.7 %all_to_all.21.packed_ref = f32[16,24,256]{2,1,0:T(8,128)S(1)} all-to-all(f32[16,24,256]{2,1,0:T(8,128)S(1)} %pack.1), channel_id=1, replica_groups=mesh['row'=16,'col'=16] {'col'}, dimensions={0} | all-to-all | bytes 786432 | tf_op jit(solution)/shard_map/all_to_all | solution.py:273
  56.4 2.8 %collective-permute-start.1 = (f32[16,8,256]{2,1,0:T(8,128)S(1)}, f32[16,8,256]{2,1,0:T(8,128)S(1)}, u32[]{:S(2)}, u32[]{:S(2)}) collective-permute-start(f32[16,8,256]{2,1,0:T(8,128)S(1)} %slice.4), channel_id=1, source_target_pairs={{0,16},{16,0},{32,48},{48,32},{64,80},{80,64},{96,112},{112,96},{1... | collective-permute-start | bytes 393224 | tf_op jit(solution)/shard_map/ppermute | solution.py:274
  59.2 1.0 %collective-permute-done.1.other_ref = f32[16,8,256]{2,1,0:T(8,128)S(1)} collective-permute-done((f32[16,8,256]{2,1,0:T(8,128)S(1)}, f32[16,8,256]{2,1,0:T(8,128)S(1)}, u32[]{:S(2)}, u32[]{:S(2)}) %collective-permute-start.1) | collective-permute-done | bytes 131104 | tf_op jit(solution)/shard_map/ppermute | solution.py:274
  60.2 6.7 %solve.1 = (f32[16,256]{1,0:T(8,128)S(1)}, f32[1,256]{1,0:T(1,128)S(1)}) custom-call(s32[1]{0:T(128)} %bitcast.core_ref, f32[16,24,256]{2,1,0:T(8,128)S(1)} %all_to_all.21.packed_ref, f32[16,8,256]{2,1,0:T(8,128)S(1)} %collective-permute-done.1.other_ref, f32[256,256]{1,0:T(8,128)S(1)} %get-tuple-element.13.gram_c_ref), custom_call_target="tpu_custom_call" | custom-call | tf_op jit(solution)/shard_map/solve/pallas_call | solution.py:225
  66.8 0.4 collective-permute-start.2
  67.3 0.8 collective-permute-done.2
  68.1 0.1 broadcast_in_dim.20
  68.2 17.7 %all_to_all.22.squares_ref = f32[128,1,256]{2,1,0:T(1,128)S(1)} all-to-all(f32[128,1,256]{2,1,0:T(1,128)S(1)} %broadcast_in_dim.20), channel_id=1, replica_groups={{0,1,2,3,4,5,6,7,8,9,10,11,12,13,14,15,32,33,34,35,36,37,38,39,40,41,42..., dimensions={0} | all-to-all | bytes 262144 | tf_op jit(solution)/shard_map/all_to_all | solution.py:282
  85.9 0.8 finish.1
  (3 shorter events, 0.0 us)
Async XLA Ops:
  22.1 3.1 %collective-permute-start = (f32[8,16,256]{2,1,0:T(8,128)S(1)}, f32[8,16,256]{2,1,0:T(8,128)S(1)}, u32[]{:S(2)}, u32[]{:S(2)}) collective-permute-start(f32[8,16,256]{2,1,0:T(8,128)S(1)} %all_to_all.20.mine_ref), channel_id=1, source_target_pairs={{0,16},{16,0},{32,48},{48,32},{64,80},{80,64},{96,112},{112,96},{1... | collective-permute-start | bytes 393224 | tf_op jit(solution)/shard_map/ppermute | solution.py:269
  26.3 13.3 %all-to-all-start.1 = ((f32[16,8,256]{2,1,0:T(8,128)}), f32[16,8,256]{2,1,0:T(8,128)S(1)}, u32[]{:S(2)}, u32[]{:S(2)}) async-start(f32[16,8,256]{2,1,0:T(8,128)} %get-tuple-element.10), calls=%async_computation.1 | async-start | bytes 262144 | tf_op jit(solution)/shard_map/all_to_all | solution.py:271
  31.8 0.8 copy-start
  56.4 3.8 %collective-permute-start.1 = (f32[16,8,256]{2,1,0:T(8,128)S(1)}, f32[16,8,256]{2,1,0:T(8,128)S(1)}, u32[]{:S(2)}, u32[]{:S(2)}) collective-permute-start(f32[16,8,256]{2,1,0:T(8,128)S(1)} %slice.4), channel_id=1, source_target_pairs={{0,16},{16,0},{32,48},{48,32},{64,80},{80,64},{96,112},{112,96},{1... | collective-permute-start | bytes 393224 | tf_op jit(solution)/shard_map/ppermute | solution.py:274
  66.8 1.3 %collective-permute-start.2 = (f32[1,256]{1,0:T(1,128)S(1)}, f32[1,256]{1,0:T(1,128)S(1)}, u32[]{:S(2)}, u32[]{:S(2)}) collective-permute-start(f32[1,256]{1,0:T(1,128)S(1)} %get-tuple-element.14), channel_id=1, source_target_pairs={{0,16},{16,0},{32,48},{48,32},{64,80},{80,64},{96,112},{112,96},{1... | collective-permute-start | bytes 3080 | tf_op jit(solution)/shard_map/ppermute | solution.py:276

commit v4 on v3

--- a/solution.py
+++ b/solution.py
@@ -27,7 +27,8 @@
     )
 
 
-def gram_kernel(core_ref, mine_ref, other_ref, block_ref, part_ref):
+def gram_kernel(core_ref, mine_ref, other_ref, c_ref, block_ref, part_ref, c_out_ref):
+    c_out_ref[...] = c_ref[...]
     mine = mine_ref[...]
     count, width, cols_j = mine.shape
     block = interleave(core_ref[0], mine, other_ref[...]).reshape(2 * count * width, cols_j)
@@ -38,7 +39,7 @@
     part_ref[...] = part.reshape(part_ref.shape)
 
 
-def partial_gram(core, mine, other, peers):
+def partial_gram(core, mine, other, factor_c, peers):
     count, width, cols_j = mine.shape
     ranks = 2 * count * width
     return pl.pallas_call(
@@ -46,13 +47,14 @@
         out_shape=(
             jax.ShapeDtypeStruct((ranks, cols_j), f32),
             jax.ShapeDtypeStruct((peers, ranks // 2 // peers, ranks), f32),
+            jax.ShapeDtypeStruct(factor_c.shape, f32),
         ),
         in_specs=[pl.BlockSpec(memory_space=pltpu.SMEM)]
-        + [pl.BlockSpec(memory_space=pltpu.VMEM)] * 2,
-        out_specs=[pl.BlockSpec(memory_space=pltpu.VMEM)] * 2,
+        + [pl.BlockSpec(memory_space=pltpu.VMEM)] * 3,
+        out_specs=[pl.BlockSpec(memory_space=pltpu.VMEM)] * 3,
         compiler_params=pltpu.CompilerParams(vmem_limit_bytes=limit),
         name="gram_part",
-    )(core, mine, other)
+    )(core, mine, other, factor_c)
 
 
 def halves(value):
@@ -60,7 +62,7 @@
     return top, (value - top.astype(f32)).astype(bf16)
 
 
-def mttkrp_kernel(slab_hbm, block_ref, c_hbm, out_ref, gram_c_ref, slab_ref, c_ref, arrived):
+def mttkrp_kernel(slab_hbm, block_ref, c_ref, out_ref, gram_c_ref, slab_ref, arrived):
     pieces = []
     first = 0
     for part, count in enumerate(frames):
@@ -68,11 +70,8 @@
         copy = pltpu.make_async_copy(slab_hbm.at[here], slab_ref.at[here], arrived.at[part])
         pieces.append((copy, range(first, first + count)))
         first += count
-    c_copy = pltpu.make_async_copy(c_hbm, c_ref, arrived.at[len(frames)])
-    c_copy.start()
     for copy, _ in pieces:
         copy.start()
-    c_copy.wait()
     c = c_ref[...]
     gram_c_ref[...] = lax.dot_general(
         c, c, (((0,), (0,)), ((), ())), precision=high, preferred_element_type=f32
@@ -100,15 +99,11 @@
             jax.ShapeDtypeStruct((rows_i, ranks), f32),
             jax.ShapeDtypeStruct((ranks, ranks), f32),
         ),
-        in_specs=[
-            pl.BlockSpec(memory_space=pl.ANY),
-            pl.BlockSpec(memory_space=pltpu.VMEM),
-            pl.BlockSpec(memory_space=pl.ANY),
-        ],
+        in_specs=[pl.BlockSpec(memory_space=pl.ANY)]
+        + [pl.BlockSpec(memory_space=pltpu.VMEM)] * 2,
         scratch_shapes=[
             pltpu.VMEM(slab.shape, f32),
-            pltpu.VMEM(factor_c.shape, f32),
-            pltpu.SemaphoreType.DMA((len(frames) + 1,)),
+            pltpu.SemaphoreType.DMA((len(frames),)),
         ],
         compiler_params=pltpu.CompilerParams(vmem_limit_bytes=wide),
         cost_estimate=pl.CostEstimate(
@@ -146,63 +141,86 @@
 
 def left_parts(value):
     top, middle, low = split(value)
-    return jnp.concatenate([top, top, middle, top, middle, low], axis=1)
+    return jnp.concatenate([top, top, middle, top, middle, low], axis=0)
 
 
 def right_parts(value):
     top, middle, low = split(value)
     return jnp.concatenate([top, middle, top, low, middle, top], axis=0)
+
+
+def spread(block, offset):
+    return [
+        jnp.broadcast_to(block[:, offset + q : offset + q + 1], block.shape) for q in range(pivots)
+    ]
+
+
+def over_rows(tile, q):
+    return jnp.broadcast_to(tile[q : q + 1], tile.shape)
 
 
 def eliminate(tiles, tile, offset):
     shape = tiles[0].shape
     row = lax.broadcasted_iota(jnp.int32, shape, 0)
     lane = lax.broadcasted_iota(jnp.int32, shape, 1) - offset
-    cols = [
-        jnp.broadcast_to(tiles[tile][:, offset + q : offset + q + 1], shape) for q in range(pivots)
-    ]
+    cols = spread(tiles[tile], offset)
+    tiles = list(tiles)
     unit = jnp.where(lane == row, 1.0, 0.0)
-    tiles = list(tiles)
     tiles[tile] = jnp.where((lane >= 0) & (lane < pivots), unit, tiles[tile])
     scale = jnp.ones(shape, f32)
     for q in range(pivots):
         here = row == q
+        if q + 1 < pivots:
+            change = jnp.where(here, 0.0, cols[q] * over_rows(cols[q + 1], q))
         inverse = jnp.broadcast_to(1.0 / cols[q][q : q + 1], shape)
         factor = jnp.where(here, 0.0, cols[q] * inverse)
         scale = jnp.where(here, inverse, scale)
-        for p in range(q + 1, pivots):
-            cols[p] = cols[p] - factor * jnp.broadcast_to(cols[p][q : q + 1], shape)
-        tiles = [part - factor * jnp.broadcast_to(part[q : q + 1], shape) for part in tiles]
+        if q + 1 < pivots:
+            cols[q + 1] = cols[q + 1] - change * inverse
+        for p in range(q + 2, pivots):
+            cols[p] = cols[p] - factor * over_rows(cols[p], q)
+        tiles = [part - factor * over_rows(part, q) for part in tiles]
     return [part * scale for part in tiles]
 
 
 def invert(gram_ref):
     size = gram_ref.shape[0]
     starts = range(0, size, lanes)
+    lane = lax.broadcasted_iota(jnp.int32, (pivots, lanes), 1)
     for k0 in range(0, size, pivots):
         k1 = k0 + pivots
         k2 = min(k1 + pivots, size)
-        tiles = [gram_ref[k0:k2, t : t + lanes] for t in starts]
-        tiles = eliminate(tiles, k0 // lanes, k0 % lanes)
-        done = jnp.concatenate([part[:pivots] for part in tiles], axis=1)
-        right = right_parts(done)
+        tile, offset = k0 // lanes, k0 % lanes
+
+        def without_block(rows, t):
+            here = lax.broadcasted_iota(jnp.int32, rows.shape, 1) - offset
+            return jnp.where((here >= 0) & (here < pivots), 0.0, rows) if t == tile else rows
+
+        head = [gram_ref[k0:k1, t : t + lanes] for t in starts]
+        signed = [jnp.where(lane < k0 - t, -part, part) for part, t in zip(head, starts)]
+        left = left_parts(jnp.concatenate(signed, axis=1))
         if k2 > k1:
-            for part, t in zip(tiles, starts):
-                gram_ref[k1:k2, t : t + lanes] = part[pivots:]
-
-        def update(first, last):
-            if first < last:
-                rows = gram_ref[first:last]
-                lane = lax.broadcasted_iota(jnp.int32, rows.shape, 1)
-                base = jnp.where((lane >= k0) & (lane < k1), 0.0, rows)
-                gram_ref[first:last] = base - jnp.dot(
-                    left_parts(rows[:, k0:k1]), right, preferred_element_type=f32
-                )
-
-        update(k2, min(k2 + pivots, size))
-        update(k2 + pivots, size)
-        update(0, k0)
-        gram_ref[k0:k1] = done
+            ahead = spread(gram_ref[k1:k2, tile * lanes : (tile + 1) * lanes], offset)
+        done = eliminate(head, tile, offset)
+        for t, part in enumerate(done):
+            here = slice(t * lanes, (t + 1) * lanes)
+            if k2 > k1:
+                sums = [ahead[q] * over_rows(part, q) for q in range(4)]
+                for q in range(4, pivots):
+                    sums[q % 4] = sums[q % 4] + ahead[q] * over_rows(part, q)
+                change = (sums[0] + sums[1]) + (sums[2] + sums[3])
+                gram_ref[k1:k2, here] = without_block(gram_ref[k1:k2, here], t) - change
+        update = lax.dot_general(
+            left, right_parts(jnp.concatenate(done, axis=1)), (((0,), (0,)), ((), ())),
+            preferred_element_type=f32,
+        )
+        for t, part in enumerate(done):
+            here = slice(t * lanes, (t + 1) * lanes)
+            for first, last in ((k2, size), (0, k0)):
+                if first < last:
+                    rows = without_block(gram_ref[first:last, here], t)
+                    gram_ref[first:last, here] = rows - update[first:last, here]
+            gram_ref[k0:k1, here] = part
 
 
 def solve_kernel(core_ref, packed_ref, other_ref, gram_c_ref, solved_ref, squares_ref, gram_ref):
@@ -267,7 +285,7 @@
     copies = jnp.broadcast_to(factor_b.T[None], (chips, width, cols_j))
     mine = lax.all_to_all(copies, "row", 0, 0, axis_index_groups=same_core)
     other = lax.ppermute(mine, "row", swap)
-    block, parts = partial_gram(core, mine, other, n_col)
+    block, parts, factor_c = partial_gram(core, mine, other, factor_c, n_col)
     parts = lax.all_to_all(parts, "col", 0, 0)
     terms, gram_c = mttkrp(tensor, block, factor_c)
     packed = lax.all_to_all(pack(parts, terms), "col", 0, 0)

time: 87.1 us -> 86.5 us (level)
  no operation moved by 1% of the time
where the time goes in v4:
time: 86.5 us; the launch traced here: 86.1 us
  blocking collectives  54.5 us (63%)
  Pallas kernels  13.5 us (16%)
  starting transfers between devices  10.9 us (13%)
  waiting for transfers between devices  5.02 us (6%)
  local copies, waits for them, and re-layouts  1.57 us (2%)
    all_to_all x1, blocking collectives, local(): mine = lax.all_to_all(copies, 'row', 0, 0, axis_index_groups=same_core)  20.8 us
    all_to_all x1, blocking collectives, local(): squares = lax.all_to_all(copies, both, 0, 0, axis_index_groups=same_core)  17.8 us
    all_to_all x1, blocking collectives, local(): packed = lax.all_to_all(pack(parts, terms), 'col', 0, 0)  16 us
    pallas_call x1, Pallas kernels, solve(): pl.pallas_call(solve_kernel, out_shape=(jax.ShapeDtypeStruct((packed.shap...  6.07 us
    pallas_call x1, Pallas kernels, mttkrp(): pl.pallas_call(mttkrp_kernel, out_shape=(jax.ShapeDtypeStruct((rows_i, ra...  5.55 us
    all_to_all x1, starting transfers between devices, local(): parts = lax.all_to_all(parts, 'col', 0, 0)  5.49 us
    ppermute x1, starting transfers between devices, local(): other = lax.ppermute(packed[:, :parts.shape[1]], 'row', swap)  2.81 us
    all_to_all x1, waiting for transfers between devices, local(): parts = lax.all_to_all(parts, 'col', 0, 0)  2.22 us
  transfers between devices with their start and end apart: 4, of which 4 were waited for; matrix products, arithmetic and copies ran while one was open for 0% of the time, Pallas kernels for 6%

profile of v4, /device:TPU:1, one launch (start us, length us, event | category | flops | bytes accessed | tf_op | source)
XLA Modules:
  0.0 86.1 jit_solution(14960619556361831543)
XLA Ops:
  0.6 0.7 broadcast_in_dim.18
  1.4 20.8 %all_to_all.20.mine_ref = f32[8,16,256]{2,1,0:T(8,128)S(1)} all-to-all(f32[8,16,256]{2,1,0:T(8,128)S(1)} %broadcast_in_dim.18), channel_id=1, replica_groups={{0,32,64,96,128,160,192,224},{16,48,80,112,144,176,208,240},{1,33,65,97..., dimensions={0} | all-to-all | bytes 262144 | tf_op jit(solution)/shard_map/all_to_all | solution.py:286
  22.1 2.1 %collective-permute-start = (f32[8,16,256]{2,1,0:T(8,128)S(1)}, f32[8,16,256]{2,1,0:T(8,128)S(1)}, u32[]{:S(2)}, u32[]{:S(2)}) collective-permute-start(f32[8,16,256]{2,1,0:T(8,128)S(1)} %all_to_all.20.mine_ref), channel_id=1, source_target_pairs={{0,16},{16,0},{32,48},{48,32},{64,80},{80,64},{96,112},{112,96},{1... | collective-permute-start | bytes 393224 | tf_op jit(solution)/shard_map/ppermute | solution.py:287
  24.2 1.0 %collective-permute-done.other_ref = f32[8,16,256]{2,1,0:T(8,128)S(1)} collective-permute-done((f32[8,16,256]{2,1,0:T(8,128)S(1)}, f32[8,16,256]{2,1,0:T(8,128)S(1)}, u32[]{:S(2)}, u32[]{:S(2)}) %collective-permute-start) | collective-permute-done | bytes 131104 | tf_op jit(solution)/shard_map/ppermute | solution.py:287
  25.2 0.0 copy-start
  25.2 0.8 copy-done
  26.0 1.1 %gram_part.1 = (f32[256,256]{1,0:T(8,128)S(1)}, f32[16,8,256]{2,1,0:T(8,128)}, f32[32,256]{1,0:T(8,128)S(1)}) custom-call(s32[1]{0:T(128)} %bitcast.core_ref, f32[8,16,256]{2,1,0:T(8,128)S(1)} %all_to_all.20.mine_ref, f32[8,16,256]{2,1,0:T(8,128)S(1)} %collective-permute-done.other_ref, f32[32,256]{1,0:T(8,128)S(1)} %copy-done), custom_call_target="tpu_custom_call" | custom-call | tf_op jit(solution)/shard_map/gram_part/pallas_call | solution.py:45
  27.0 5.5 %all-to-all-start.1 = ((f32[16,8,256]{2,1,0:T(8,128)}), f32[16,8,256]{2,1,0:T(8,128)S(1)}, u32[]{:S(2)}, u32[]{:S(2)}) async-start(f32[16,8,256]{2,1,0:T(8,128)} %get-tuple-element.11), calls=%async_computation.1 | async-start | bytes 262144 | tf_op jit(solution)/shard_map/all_to_all | solution.py:289
  32.5 5.5 %mttkrp.1 = (f32[256,256]{1,0:T(8,128)S(1)}, f32[256,256]{1,0:T(8,128)S(1)}) custom-call(f32[32,256,256]{2,1,0:T(8,128)} %slab_hbm.1, f32[256,256]{1,0:T(8,128)S(1)} %get-tuple-element.12.block_ref, f32[32,256]{1,0:T(8,128)S(1)} %get-tuple-element.13.c_ref), custom_call_target="tpu_custom_call" | custom-call | flops 3221225472 | bytes 8388608 | tf_op jit(solution)/shard_map/mttkrp/pallas_call | solution.py:96
  38.1 2.2 %all-to-all-done.1.parts_ref = f32[16,8,256]{2,1,0:T(8,128)S(1)} async-done(((f32[16,8,256]{2,1,0:T(8,128)}), f32[16,8,256]{2,1,0:T(8,128)S(1)}, u32[]{:S(2)}, u32[]{:S(2)}) %all-to-all-start.1) | async-done | bytes 131104 | tf_op jit(solution)/shard_map/all_to_all | solution.py:289
  40.4 16.0 %all_to_all.21.packed_ref = f32[16,24,256]{2,1,0:T(8,128)S(1)} all-to-all(f32[16,24,256]{2,1,0:T(8,128)S(1)} %pack.1), channel_id=1, replica_groups=mesh['row'=16,'col'=16] {'col'}, dimensions={0} | all-to-all | bytes 786432 | tf_op jit(solution)/shard_map/all_to_all | solution.py:291
  56.3 2.8 %collective-permute-start.1 = (f32[16,8,256]{2,1,0:T(8,128)S(1)}, f32[16,8,256]{2,1,0:T(8,128)S(1)}, u32[]{:S(2)}, u32[]{:S(2)}) collective-permute-start(f32[16,8,256]{2,1,0:T(8,128)S(1)} %slice.4), channel_id=1, source_target_pairs={{0,16},{16,0},{32,48},{48,32},{64,80},{80,64},{96,112},{112,96},{1... | collective-permute-start | bytes 393224 | tf_op jit(solution)/shard_map/ppermute | solution.py:292
  59.1 1.0 %collective-permute-done.1.other_ref = f32[16,8,256]{2,1,0:T(8,128)S(1)} collective-permute-done((f32[16,8,256]{2,1,0:T(8,128)S(1)}, f32[16,8,256]{2,1,0:T(8,128)S(1)}, u32[]{:S(2)}, u32[]{:S(2)}) %collective-permute-start.1) | collective-permute-done | bytes 131104 | tf_op jit(solution)/shard_map/ppermute | solution.py:292
  60.1 6.1 %solve.1 = (f32[16,256]{1,0:T(8,128)S(1)}, f32[1,256]{1,0:T(1,128)S(1)}) custom-call(s32[1]{0:T(128)} %bitcast.core_ref, f32[16,24,256]{2,1,0:T(8,128)S(1)} %all_to_all.21.packed_ref, f32[16,8,256]{2,1,0:T(8,128)S(1)} %collective-permute-done.1.other_ref, f32[256,256]{1,0:T(8,128)S(1)} %get-tuple-element.15.gram_c_ref), custom_call_target="tpu_custom_call" | custom-call | tf_op jit(solution)/shard_map/solve/pallas_call | solution.py:243
  66.2 0.4 collective-permute-start.2
  66.7 0.8 collective-permute-done.2
  67.5 0.1 broadcast_in_dim.20
  67.6 17.8 %all_to_all.22.squares_ref = f32[128,1,256]{2,1,0:T(1,128)S(1)} all-to-all(f32[128,1,256]{2,1,0:T(1,128)S(1)} %broadcast_in_dim.20), channel_id=1, replica_groups={{0,1,2,3,4,5,6,7,8,9,10,11,12,13,14,15,32,33,34,35,36,37,38,39,40,41,42..., dimensions={0} | all-to-all | bytes 262144 | tf_op jit(solution)/shard_map/all_to_all | solution.py:300
  85.3 0.8 finish.1
  (3 shorter events, 0.0 us)
Async XLA Ops:
  22.1 3.1 %collective-permute-start = (f32[8,16,256]{2,1,0:T(8,128)S(1)}, f32[8,16,256]{2,1,0:T(8,128)S(1)}, u32[]{:S(2)}, u32[]{:S(2)}) collective-permute-start(f32[8,16,256]{2,1,0:T(8,128)S(1)} %all_to_all.20.mine_ref), channel_id=1, source_target_pairs={{0,16},{16,0},{32,48},{48,32},{64,80},{80,64},{96,112},{112,96},{1... | collective-permute-start | bytes 393224 | tf_op jit(solution)/shard_map/ppermute | solution.py:287
  25.2 0.8 copy-start
  27.0 13.3 %all-to-all-start.1 = ((f32[16,8,256]{2,1,0:T(8,128)}), f32[16,8,256]{2,1,0:T(8,128)S(1)}, u32[]{:S(2)}, u32[]{:S(2)}) async-start(f32[16,8,256]{2,1,0:T(8,128)} %get-tuple-element.11), calls=%async_computation.1 | async-start | bytes 262144 | tf_op jit(solution)/shard_map/all_to_all | solution.py:289
  56.3 3.8 %collective-permute-start.1 = (f32[16,8,256]{2,1,0:T(8,128)S(1)}, f32[16,8,256]{2,1,0:T(8,128)S(1)}, u32[]{:S(2)}, u32[]{:S(2)}) collective-permute-start(f32[16,8,256]{2,1,0:T(8,128)S(1)} %slice.4), channel_id=1, source_target_pairs={{0,16},{16,0},{32,48},{48,32},{64,80},{80,64},{96,112},{112,96},{1... | collective-permute-start | bytes 393224 | tf_op jit(solution)/shard_map/ppermute | solution.py:292
  66.2 1.3 %collective-permute-start.2 = (f32[1,256]{1,0:T(1,128)S(1)}, f32[1,256]{1,0:T(1,128)S(1)}, u32[]{:S(2)}, u32[]{:S(2)}) collective-permute-start(f32[1,256]{1,0:T(1,128)S(1)} %get-tuple-element.16), channel_id=1, source_target_pairs={{0,16},{16,0},{32,48},{48,32},{64,80},{80,64},{96,112},{112,96},{1... | collective-permute-start | bytes 3080 | tf_op jit(solution)/shard_map/ppermute | solution.py:294

commit v5 on v4

--- a/solution.py
+++ b/solution.py
@@ -13,6 +13,7 @@
 bf16 = jnp.bfloat16
 limit = 16 * 1024 * 1024
 wide = 52 * 1024 * 1024
+beside = 10**10
 pivots = 16
 lanes = 128
 frames = (4, 12, 16)
@@ -20,26 +21,15 @@
 nt = (((1,), (1,)), ((), ()))
 
 
-def interleave(core, mine, other):
-    first = core == 0
-    return jnp.concatenate(
-        [jnp.where(first, mine, other), jnp.where(first, other, mine)], axis=1
-    )
-
-
-def gram_kernel(core_ref, mine_ref, other_ref, c_ref, block_ref, part_ref, c_out_ref):
-    c_out_ref[...] = c_ref[...]
-    mine = mine_ref[...]
-    count, width, cols_j = mine.shape
-    block = interleave(core_ref[0], mine, other_ref[...]).reshape(2 * count * width, cols_j)
-    block_ref[...] = block
-    part = lax.dot_general(
-        mine.reshape(count * width, cols_j), block, nt, precision=high, preferred_element_type=f32
-    )
+def gram_kernel(mine_ref, other_ref, block_ref, part_ref):
+    mine = mine_ref[...].reshape(part_ref.shape[0] * part_ref.shape[1], block_ref.shape[1])
+    block_ref[: mine.shape[0]] = mine
+    block_ref[mine.shape[0] :] = other_ref[...].reshape(mine.shape)
+    part = lax.dot_general(mine, block_ref[...], nt, precision=high, preferred_element_type=f32)
     part_ref[...] = part.reshape(part_ref.shape)
 
 
-def partial_gram(core, mine, other, factor_c, peers):
+def partial_gram(mine, other, peers):
     count, width, cols_j = mine.shape
     ranks = 2 * count * width
     return pl.pallas_call(
@@ -47,14 +37,35 @@
         out_shape=(
             jax.ShapeDtypeStruct((ranks, cols_j), f32),
             jax.ShapeDtypeStruct((peers, ranks // 2 // peers, ranks), f32),
-            jax.ShapeDtypeStruct(factor_c.shape, f32),
-        ),
-        in_specs=[pl.BlockSpec(memory_space=pltpu.SMEM)]
-        + [pl.BlockSpec(memory_space=pltpu.VMEM)] * 3,
-        out_specs=[pl.BlockSpec(memory_space=pltpu.VMEM)] * 3,
-        compiler_params=pltpu.CompilerParams(vmem_limit_bytes=limit),
+        ),
+        compiler_params=pltpu.CompilerParams(vmem_limit_bytes=limit),
+        cost_estimate=pl.CostEstimate(
+            flops=beside, bytes_accessed=8 * ranks * cols_j, transcendentals=0
+        ),
         name="gram_part",
-    )(core, mine, other, factor_c)
+    )(mine, other)
+
+
+def own_first(core, value):
+    front, back = value[:, :lanes], value[:, lanes:]
+    lane = lax.broadcasted_iota(jnp.int32, front.shape, 1)
+    tiles = []
+    for whose in (core, 1 - core):
+        index = 32 * (lane // 16 % 4) + 16 * whose + lane % 16
+        low, top = (jnp.take_along_axis(part, index, axis=1) for part in (front, back))
+        tiles.append(jnp.where(lane < lanes // 2, low, top))
+    return jnp.concatenate(tiles, axis=1)
+
+
+def by_turns(core, value):
+    own, other = value[:, :lanes], value[:, lanes:]
+    lane = lax.broadcasted_iota(jnp.int32, own.shape, 1)
+    tiles = []
+    for t in range(2):
+        index = 16 * (4 * t + lane // 32) + lane % 16
+        ours, theirs = (jnp.take_along_axis(part, index, axis=1) for part in (own, other))
+        tiles.append(jnp.where(lane // 16 % 2 == core, ours, theirs))
+    return jnp.concatenate(tiles, axis=1)
 
 
 def halves(value):
@@ -62,7 +73,7 @@
     return top, (value - top.astype(f32)).astype(bf16)
 
 
-def mttkrp_kernel(slab_hbm, block_ref, c_ref, out_ref, gram_c_ref, slab_ref, arrived):
+def mttkrp_kernel(core_ref, slab_hbm, block_ref, c_ref, out_ref, gram_c_ref, slab_ref, arrived):
     pieces = []
     first = 0
     for part, count in enumerate(frames):
@@ -72,7 +83,7 @@
         first += count
     for copy, _ in pieces:
         copy.start()
-    c = c_ref[...]
+    c = own_first(core_ref[0], c_ref[...])
     gram_c_ref[...] = lax.dot_general(
         c, c, (((0,), (0,)), ((), ())), precision=high, preferred_element_type=f32
     )
@@ -90,7 +101,7 @@
     out_ref[...] = total
 
 
-def mttkrp(slab, block, factor_c):
+def mttkrp(core, slab, block, factor_c):
     depth, rows_i, cols_j = slab.shape
     ranks = block.shape[0]
     return pl.pallas_call(
@@ -99,7 +110,7 @@
             jax.ShapeDtypeStruct((rows_i, ranks), f32),
             jax.ShapeDtypeStruct((ranks, ranks), f32),
         ),
-        in_specs=[pl.BlockSpec(memory_space=pl.ANY)]
+        in_specs=[pl.BlockSpec(memory_space=pltpu.SMEM), pl.BlockSpec(memory_space=pl.ANY)]
         + [pl.BlockSpec(memory_space=pltpu.VMEM)] * 2,
         scratch_shapes=[
             pltpu.VMEM(slab.shape, f32),
@@ -112,7 +123,7 @@
             transcendentals=0,
         ),
         name="mttkrp",
-    )(slab, block, factor_c)
+    )(core, slab, block, factor_c)
 
 
 def pack_kernel(parts_ref, terms_ref, out_ref):
@@ -183,11 +194,11 @@
     return [part * scale for part in tiles]
 
 
-def invert(gram_ref):
-    size = gram_ref.shape[0]
-    starts = range(0, size, lanes)
+def invert(gram_ref, begin, end):
+    size, ranks = gram_ref.shape
+    starts = range(0, ranks, lanes)
     lane = lax.broadcasted_iota(jnp.int32, (pivots, lanes), 1)
-    for k0 in range(0, size, pivots):
+    for k0 in range(begin, end, pivots):
         k1 = k0 + pivots
         k2 = min(k1 + pivots, size)
         tile, offset = k0 // lanes, k0 % lanes
@@ -198,7 +209,7 @@
 
         head = [gram_ref[k0:k1, t : t + lanes] for t in starts]
         signed = [jnp.where(lane < k0 - t, -part, part) for part, t in zip(head, starts)]
-        left = left_parts(jnp.concatenate(signed, axis=1))
+        left = left_parts(jnp.concatenate(signed[: size // lanes], axis=1))
         if k2 > k1:
             ahead = spread(gram_ref[k1:k2, tile * lanes : (tile + 1) * lanes], offset)
         done = eliminate(head, tile, offset)
@@ -223,22 +234,49 @@
             gram_ref[k0:k1, here] = part
 
 
-def solve_kernel(core_ref, packed_ref, other_ref, gram_c_ref, solved_ref, squares_ref, gram_ref):
-    other = other_ref[...]
-    peers, rows, ranks = other.shape
-    shape = (peers // 2, 2 * rows, ranks)
-    gram_b = interleave(
-        core_ref[0], packed_ref[:, :rows].reshape(shape), other.reshape(shape)
-    ).reshape(ranks, ranks)
-    gram_ref[...] = gram_b * gram_c_ref[...]
-    invert(gram_ref)
+def first_kernel(packed_ref, gram_c_ref, own_ref, change_ref):
+    half, ranks = own_ref.shape
+    rows = half // packed_ref.shape[0]
+    own = packed_ref[:, :rows].reshape(half, ranks) * gram_c_ref[:half]
+    own_ref[...] = own
+    left = left_parts(own[:, half:])
+    invert(own_ref, 0, half)
+    change_ref[...] = lax.dot_general(
+        left, right_parts(own_ref[...]), (((0,), (0,)), ((), ())), preferred_element_type=f32
+    )
+
+
+def first_half(packed, gram_c):
+    half = jax.ShapeDtypeStruct((gram_c.shape[0] // 2, gram_c.shape[1]), f32)
+    return pl.pallas_call(
+        first_kernel,
+        out_shape=(half, half),
+        compiler_params=pltpu.CompilerParams(vmem_limit_bytes=limit),
+        cost_estimate=pl.CostEstimate(
+            flops=beside, bytes_accessed=packed.size * 4, transcendentals=0
+        ),
+        name="first_half",
+    )(packed, gram_c)
+
+
+def solve_kernel(
+    core_ref, own_ref, change_ref, packed_ref, other_ref, gram_c_ref, solved_ref, squares_ref, gram_ref
+):
+    half, ranks = own_ref.shape
+    rows = other_ref.shape[1]
+    gram_ref[:half] = own_ref[...]
+    other = other_ref[...].reshape(half, ranks)[:, :half] * gram_c_ref[half:, half:]
+    gram_ref[half:, :half] = -change_ref[:, :half]
+    gram_ref[half:, half:] = other - change_ref[:, half:]
+    invert(gram_ref, half, ranks)
     mine = jnp.sum(packed_ref[:, rows:], axis=0)
     solved = jnp.dot(mine, gram_ref[...], precision=high, preferred_element_type=f32)
+    solved = by_turns(core_ref[0], solved)
     solved_ref[...] = solved
     squares_ref[...] = jnp.sum(solved * solved, axis=0, keepdims=True)
 
 
-def solve(core, packed, other, gram_c):
+def solve(core, own, change, packed, other, gram_c):
     peers, rows, ranks = other.shape
     return pl.pallas_call(
         solve_kernel,
@@ -247,11 +285,11 @@
             jax.ShapeDtypeStruct((1, ranks), f32),
         ),
         in_specs=[pl.BlockSpec(memory_space=pltpu.SMEM)]
-        + [pl.BlockSpec(memory_space=pltpu.VMEM)] * 3,
+        + [pl.BlockSpec(memory_space=pltpu.VMEM)] * 5,
         scratch_shapes=[pltpu.VMEM((ranks, ranks), f32)],
         compiler_params=pltpu.CompilerParams(vmem_limit_bytes=limit),
         name="solve",
-    )(core, packed, other, gram_c)
+    )(core, own, change, packed, other, gram_c)
 
 
 def finish_kernel(count, squares_ref, solved_ref, factor_ref, scale_ref):
@@ -285,12 +323,13 @@
     copies = jnp.broadcast_to(factor_b.T[None], (chips, width, cols_j))
     mine = lax.all_to_all(copies, "row", 0, 0, axis_index_groups=same_core)
     other = lax.ppermute(mine, "row", swap)
-    block, parts, factor_c = partial_gram(core, mine, other, factor_c, n_col)
+    block, parts = partial_gram(mine, other, n_col)
     parts = lax.all_to_all(parts, "col", 0, 0)
-    terms, gram_c = mttkrp(tensor, block, factor_c)
+    terms, gram_c = mttkrp(core, tensor, block, factor_c)
     packed = lax.all_to_all(pack(parts, terms), "col", 0, 0)
     other = lax.ppermute(packed[:, : parts.shape[1]], "row", swap)
-    solved, squares = solve(core, packed, other, gram_c)
+    own, change = first_half(packed, gram_c)
+    solved, squares = solve(core, own, change, packed, other, gram_c)
     squares = squares + lax.ppermute(squares, "row", swap)
     same_core = [
         [(2 * chip + core) * n_col + c for chip in range(chips) for c in range(n_col)]

time: 86.5 us -> 84.8 us (0.980)
    pallas_call x0 -> x1, Pallas kernels: none -> 3.09 us  [first_half(): pl.pallas_call(first_kernel, out_shape=(half, half), compiler_params=pltp...]
    pallas_call x1, Pallas kernels: 6.07 us -> 3.29 us  [solve(): pl.pallas_call(solve_kernel, out_shape=(jax.ShapeDtypeStruct((packed.shap...]
    ppermute x1, waiting for transfers between devices: 0.99 us -> 0.01 us  [local(): other = lax.ppermute(packed[:, :parts.shape[1]], 'row', swap)]
  transfers between devices with their start and end apart: 4 -> 4, of which waited for: 4 -> 3; matrix products, arithmetic and copies ran while one was open for 0% -> 0% of each run, Pallas kernels for 6% -> 10%
where the time goes in v5:
time: 84.8 us; the launch traced here: 84.4 us
  blocking collectives  54.3 us (64%)
  Pallas kernels  13.8 us (16%)
  starting transfers between devices  10.5 us (12%)
  waiting for transfers between devices  4.33 us (5%)
    all_to_all x1, blocking collectives, local(): mine = lax.all_to_all(copies, 'row', 0, 0, axis_index_groups=same_core)  20.8 us
    all_to_all x1, blocking collectives, local(): squares = lax.all_to_all(copies, both, 0, 0, axis_index_groups=same_core)  17.6 us
    all_to_all x1, blocking collectives, local(): packed = lax.all_to_all(pack(parts, terms), 'col', 0, 0)  16 us
    pallas_call x1, Pallas kernels, mttkrp(): pl.pallas_call(mttkrp_kernel, out_shape=(jax.ShapeDtypeStruct((rows_i, ra...  5.54 us
    all_to_all x1, starting transfers between devices, local(): parts = lax.all_to_all(parts, 'col', 0, 0)  5.49 us
    pallas_call x1, Pallas kernels, solve(): pl.pallas_call(solve_kernel, out_shape=(jax.ShapeDtypeStruct((packed.shap...  3.29 us
    pallas_call x1, Pallas kernels, first_half(): pl.pallas_call(first_kernel, out_shape=(half, half), compiler_params=pltp...  3.09 us
    ppermute x1, starting transfers between devices, local(): other = lax.ppermute(packed[:, :parts.shape[1]], 'row', swap)  2.82 us
  transfers between devices with their start and end apart: 4, of which 3 were waited for; matrix products, arithmetic and copies ran while one was open for 0% of the time, Pallas kernels for 10%

profile of v5, /device:TPU:1, one launch (start us, length us, event | category | flops | bytes accessed | tf_op | source)
XLA Modules:
  0.0 84.4 jit_solution(2065221707019879595)
XLA Ops:
  0.6 0.7 broadcast_in_dim.18
  1.4 20.8 %all_to_all.20.mine_ref = f32[8,16,256]{2,1,0:T(8,128)S(1)} all-to-all(f32[8,16,256]{2,1,0:T(8,128)S(1)} %broadcast_in_dim.18), channel_id=1, replica_groups={{0,32,64,96,128,160,192,224},{16,48,80,112,144,176,208,240},{1,33,65,97..., dimensions={0} | all-to-all | bytes 262144 | tf_op jit(solution)/shard_map/all_to_all | solution.py:324
  22.1 2.1 %collective-permute-start = (f32[8,16,256]{2,1,0:T(8,128)S(1)}, f32[8,16,256]{2,1,0:T(8,128)S(1)}, u32[]{:S(2)}, u32[]{:S(2)}) collective-permute-start(f32[8,16,256]{2,1,0:T(8,128)S(1)} %all_to_all.20.mine_ref), channel_id=1, source_target_pairs={{0,16},{16,0},{32,48},{48,32},{64,80},{80,64},{96,112},{112,96},{1... | collective-permute-start | bytes 393224 | tf_op jit(solution)/shard_map/ppermute | solution.py:325
  24.2 0.0 copy-start
  24.2 1.0 %collective-permute-done.other_ref = f32[8,16,256]{2,1,0:T(8,128)S(1)} collective-permute-done((f32[8,16,256]{2,1,0:T(8,128)S(1)}, f32[8,16,256]{2,1,0:T(8,128)S(1)}, u32[]{:S(2)}, u32[]{:S(2)}) %collective-permute-start) | collective-permute-done | bytes 131104 | tf_op jit(solution)/shard_map/ppermute | solution.py:325
  25.2 1.1 %gram_part.1 = (f32[256,256]{1,0:T(8,128)S(1)}, f32[16,8,256]{2,1,0:T(8,128)}) custom-call(f32[8,16,256]{2,1,0:T(8,128)S(1)} %all_to_all.20.mine_ref, f32[8,16,256]{2,1,0:T(8,128)S(1)} %collective-permute-done.other_ref), custom_call_target="tpu_custom_call" | custom-call | flops 10000000000 | bytes 524288 | tf_op jit(solution)/shard_map/gram_part/pallas_call | solution.py:35
  26.3 5.5 %all-to-all-start.1 = ((f32[16,8,256]{2,1,0:T(8,128)}), f32[16,8,256]{2,1,0:T(8,128)S(1)}, u32[]{:S(2)}, u32[]{:S(2)}) async-start(f32[16,8,256]{2,1,0:T(8,128)} %get-tuple-element.12), calls=%async_computation.1 | async-start | bytes 262144 | tf_op jit(solution)/shard_map/all_to_all | solution.py:327
  31.8 0.0 copy-done
  31.8 5.5 %mttkrp.1 = (f32[256,256]{1,0:T(8,128)S(1)}, f32[256,256]{1,0:T(8,128)S(1)}) custom-call(s32[1]{0:T(128)} %bitcast.core_ref, f32[32,256,256]{2,1,0:T(8,128)} %slab_hbm.1, f32[256,256]{1,0:T(8,128)S(1)} %get-tuple-element.13.block_ref, f32[32,256]{1,0:T(8,128)S(1)} %copy-done), custom_call_target="tpu_custom_call" | custom-call | flops 3221225472 | bytes 8388608 | tf_op jit(solution)/shard_map/mttkrp/pallas_call | solution.py:107
  37.3 2.2 %all-to-all-done.1.parts_ref = f32[16,8,256]{2,1,0:T(8,128)S(1)} async-done(((f32[16,8,256]{2,1,0:T(8,128)}), f32[16,8,256]{2,1,0:T(8,128)S(1)}, u32[]{:S(2)}, u32[]{:S(2)}) %all-to-all-start.1) | async-done | bytes 131104 | tf_op jit(solution)/shard_map/all_to_all | solution.py:327
  39.6 16.0 %all_to_all.21.packed_ref = f32[16,24,256]{2,1,0:T(8,128)S(1)} all-to-all(f32[16,24,256]{2,1,0:T(8,128)S(1)} %pack.1), channel_id=1, replica_groups=mesh['row'=16,'col'=16] {'col'}, dimensions={0} | all-to-all | bytes 786432 | tf_op jit(solution)/shard_map/all_to_all | solution.py:329
  55.6 2.8 %collective-permute-start.1 = (f32[16,8,256]{2,1,0:T(8,128)S(1)}, f32[16,8,256]{2,1,0:T(8,128)S(1)}, u32[]{:S(2)}, u32[]{:S(2)}) collective-permute-start(f32[16,8,256]{2,1,0:T(8,128)S(1)} %slice.4), channel_id=1, source_target_pairs={{0,16},{16,0},{32,48},{48,32},{64,80},{80,64},{96,112},{112,96},{1... | collective-permute-start | bytes 393224 | tf_op jit(solution)/shard_map/ppermute | solution.py:330
  58.4 3.1 %first_half.1 = (f32[128,256]{1,0:T(8,128)S(1)}, f32[128,256]{1,0:T(8,128)S(1)}) custom-call(f32[16,24,256]{2,1,0:T(8,128)S(1)} %all_to_all.21.packed_ref, f32[256,256]{1,0:T(8,128)S(1)} %get-tuple-element.15.gram_c_ref), custom_call_target="tpu_custom_call" | custom-call | flops 10000000000 | bytes 393216 | tf_op jit(solution)/shard_map/first_half/pallas_call | solution.py:251
  61.5 0.0 collective-permute-done.1.other_ref
  61.5 3.3 %solve.1 = (f32[16,256]{1,0:T(8,128)S(1)}, f32[1,256]{1,0:T(1,128)S(1)}) custom-call(s32[1]{0:T(128)} %bitcast.core_ref, f32[128,256]{1,0:T(8,128)S(1)} %get-tuple-element.16.own_ref, f32[128,256]{1,0:T(8,128)S(1)} %get-tuple-element.17.change_ref, f32[16,24,256]{2,1,0:T(8,128)S(1)} %all_to_all.21.packed_ref, ...), custom_call_target="tpu_custom_call" | custom-call | tf_op jit(solution)/shard_map/solve/pallas_call | solution.py:281
  64.8 0.1 collective-permute-start.2
  64.9 1.1 %collective-permute-done.2 = f32[1,256]{1,0:T(1,128)S(1)} collective-permute-done((f32[1,256]{1,0:T(1,128)S(1)}, f32[1,256]{1,0:T(1,128)S(1)}, u32[]{:S(2)}, u32[]{:S(2)}) %collective-permute-start.2) | collective-permute-done | bytes 1056 | tf_op jit(solution)/shard_map/ppermute | solution.py:333
  66.0 0.1 broadcast_in_dim.20
  66.1 17.6 %all_to_all.22.squares_ref = f32[128,1,256]{2,1,0:T(1,128)S(1)} all-to-all(f32[128,1,256]{2,1,0:T(1,128)S(1)} %broadcast_in_dim.20), channel_id=1, replica_groups={{0,1,2,3,4,5,6,7,8,9,10,11,12,13,14,15,32,33,34,35,36,37,38,39,40,41,42..., dimensions={0} | all-to-all | bytes 262144 | tf_op jit(solution)/shard_map/all_to_all | solution.py:339
  83.7 0.8 finish.1
  (3 shorter events, 0.0 us)
Async XLA Ops:
  22.1 3.1 %collective-permute-start = (f32[8,16,256]{2,1,0:T(8,128)S(1)}, f32[8,16,256]{2,1,0:T(8,128)S(1)}, u32[]{:S(2)}, u32[]{:S(2)}) collective-permute-start(f32[8,16,256]{2,1,0:T(8,128)S(1)} %all_to_all.20.mine_ref), channel_id=1, source_target_pairs={{0,16},{16,0},{32,48},{48,32},{64,80},{80,64},{96,112},{112,96},{1... | collective-permute-start | bytes 393224 | tf_op jit(solution)/shard_map/ppermute | solution.py:325
  24.2 7.5 %copy-start = (f32[32,256]{1,0:T(8,128)S(1)}, f32[32,256]{1,0:T(8,128)}, u32[]{:S(2)}) copy-start(f32[32,256]{1,0:T(8,128)} %c_ref.1) | copy-start | bytes 98308
  26.3 13.3 %all-to-all-start.1 = ((f32[16,8,256]{2,1,0:T(8,128)}), f32[16,8,256]{2,1,0:T(8,128)S(1)}, u32[]{:S(2)}, u32[]{:S(2)}) async-start(f32[16,8,256]{2,1,0:T(8,128)} %get-tuple-element.12), calls=%async_computation.1 | async-start | bytes 262144 | tf_op jit(solution)/shard_map/all_to_all | solution.py:327
  55.6 5.9 %collective-permute-start.1 = (f32[16,8,256]{2,1,0:T(8,128)S(1)}, f32[16,8,256]{2,1,0:T(8,128)S(1)}, u32[]{:S(2)}, u32[]{:S(2)}) collective-permute-start(f32[16,8,256]{2,1,0:T(8,128)S(1)} %slice.4), channel_id=1, source_target_pairs={{0,16},{16,0},{32,48},{48,32},{64,80},{80,64},{96,112},{112,96},{1... | collective-permute-start | bytes 393224 | tf_op jit(solution)/shard_map/ppermute | solution.py:330
  64.8 1.2 %collective-permute-start.2 = (f32[1,256]{1,0:T(1,128)S(1)}, f32[1,256]{1,0:T(1,128)S(1)}, u32[]{:S(2)}, u32[]{:S(2)}) collective-permute-start(f32[1,256]{1,0:T(1,128)S(1)} %get-tuple-element.18), channel_id=1, source_target_pairs={{0,16},{16,0},{32,48},{48,32},{64,80},{80,64},{96,112},{112,96},{1... | collective-permute-start | bytes 3080 | tf_op jit(solution)/shard_map/ppermute | solution.py:333

commit v6 on v5

--- a/solution.py
+++ b/solution.py
@@ -21,15 +21,39 @@
 nt = (((1,), (1,)), ((), ()))
 
 
-def gram_kernel(mine_ref, other_ref, block_ref, part_ref):
-    mine = mine_ref[...].reshape(part_ref.shape[0] * part_ref.shape[1], block_ref.shape[1])
-    block_ref[: mine.shape[0]] = mine
-    block_ref[mine.shape[0] :] = other_ref[...].reshape(mine.shape)
-    part = lax.dot_general(mine, block_ref[...], nt, precision=high, preferred_element_type=f32)
-    part_ref[...] = part.reshape(part_ref.shape)
-
-
-def partial_gram(mine, other, peers):
+def rank_gram(left, right):
+    return lax.dot_general(left, right, nt, precision=high, preferred_element_type=f32)
+
+
+def own_kernel(mine_ref, own_ref):
+    mine = mine_ref[...].reshape(own_ref.shape[0], mine_ref.shape[2])
+    own_ref[...] = rank_gram(mine, mine)
+
+
+def own_gram(mine):
+    half = mine.shape[0] * mine.shape[1]
+    return pl.pallas_call(
+        own_kernel,
+        out_shape=jax.ShapeDtypeStruct((half, half), f32),
+        compiler_params=pltpu.CompilerParams(vmem_limit_bytes=limit),
+        cost_estimate=pl.CostEstimate(
+            flops=beside, bytes_accessed=4 * mine.size, transcendentals=0
+        ),
+        name="gram_own",
+    )(mine)
+
+
+def gram_kernel(mine_ref, other_ref, own_ref, block_ref, part_ref):
+    half = own_ref.shape[0]
+    mine = mine_ref[...].reshape(half, block_ref.shape[1])
+    other = other_ref[...].reshape(mine.shape)
+    block_ref[:half] = mine
+    block_ref[half:] = other
+    part_ref[:, :, :half] = own_ref[...].reshape(part_ref.shape[:2] + (half,))
+    part_ref[:, :, half:] = rank_gram(mine, other).reshape(part_ref.shape[:2] + (half,))
+
+
+def partial_gram(mine, other, own, peers):
     count, width, cols_j = mine.shape
     ranks = 2 * count * width
     return pl.pallas_call(
@@ -43,7 +67,7 @@
             flops=beside, bytes_accessed=8 * ranks * cols_j, transcendentals=0
         ),
         name="gram_part",
-    )(mine, other)
+    )(mine, other, own)
 
 
 def own_first(core, value):
@@ -179,16 +203,20 @@
     unit = jnp.where(lane == row, 1.0, 0.0)
     tiles[tile] = jnp.where((lane >= 0) & (lane < pivots), unit, tiles[tile])
     scale = jnp.ones(shape, f32)
+    pivot = over_rows(cols[0], 0)
     for q in range(pivots):
         here = row == q
+        inverse = 1.0 / pivot
+        near = range(q + 1, min(q + 1 + 1, pivots))
+        masked = jnp.where(here, 0.0, cols[q])
+        change = [masked * over_rows(cols[p], q) for p in near]
         if q + 1 < pivots:
-            change = jnp.where(here, 0.0, cols[q] * over_rows(cols[q + 1], q))
-        inverse = jnp.broadcast_to(1.0 / cols[q][q : q + 1], shape)
-        factor = jnp.where(here, 0.0, cols[q] * inverse)
+            pivot = over_rows(cols[q + 1], q + 1) - over_rows(change[0], q + 1) * inverse
+        factor = masked * inverse
         scale = jnp.where(here, inverse, scale)
-        if q + 1 < pivots:
-            cols[q + 1] = cols[q + 1] - change * inverse
-        for p in range(q + 2, pivots):
+        for p, term in zip(near, change):
+            cols[p] = cols[p] - term * inverse
+        for p in range(q + 1 + 1, pivots):
             cols[p] = cols[p] - factor * over_rows(cols[p], q)
         tiles = [part - factor * over_rows(part, q) for part in tiles]
     return [part * scale for part in tiles]
@@ -323,7 +351,7 @@
     copies = jnp.broadcast_to(factor_b.T[None], (chips, width, cols_j))
     mine = lax.all_to_all(copies, "row", 0, 0, axis_index_groups=same_core)
     other = lax.ppermute(mine, "row", swap)
-    block, parts = partial_gram(mine, other, n_col)
+    block, parts = partial_gram(mine, other, own_gram(mine), n_col)
     parts = lax.all_to_all(parts, "col", 0, 0)
     terms, gram_c = mttkrp(core, tensor, block, factor_c)
     packed = lax.all_to_all(pack(parts, terms), "col", 0, 0)

time: 84.8 us -> 85.6 us (level)
  blocking collectives: 54.3 us -> 33.5 us
  starting transfers between devices: 10.5 us -> 22.2 us
  waiting for transfers between devices: 4.33 us -> 13.4 us
    all_to_all x1 -> x0, blocking collectives: 20.8 us -> none  [local(): mine = lax.all_to_all(copies, 'row', 0, 0, axis_index_groups=same_core)]
    all_to_all x0 -> x1, starting transfers between devices: none -> 11.6 us  [local(): mine = lax.all_to_all(copies, 'row', 0, 0, axis_index_groups=same_core)]
    all_to_all x0 -> x1, waiting for transfers between devices: none -> 9.34 us  [local(): mine = lax.all_to_all(copies, 'row', 0, 0, axis_index_groups=same_core)]
  transfers between devices with their start and end apart: 4 -> 5, of which waited for: 3 -> 4; matrix products, arithmetic and copies ran while one was open for 0% -> 0% of each run, Pallas kernels for 10% -> 10%
where the time goes in v6:
time: 85.6 us; the launch traced here: 85.1 us
  blocking collectives  33.5 us (39%)
  starting transfers between devices  22.2 us (26%)
  Pallas kernels  13.9 us (16%)
  waiting for transfers between devices  13.4 us (16%)
  local copies, waits for them, and re-layouts  1.46 us (2%)
    all_to_all x1, blocking collectives, local(): squares = lax.all_to_all(copies, both, 0, 0, axis_index_groups=same_core)  17.6 us
    all_to_all x1, blocking collectives, local(): packed = lax.all_to_all(pack(parts, terms), 'col', 0, 0)  16 us
    all_to_all x1, starting transfers between devices, local(): mine = lax.all_to_all(copies, 'row', 0, 0, axis_index_groups=same_core)  11.6 us
    all_to_all x1, waiting for transfers between devices, local(): mine = lax.all_to_all(copies, 'row', 0, 0, axis_index_groups=same_core)  9.34 us
    pallas_call x1, Pallas kernels, mttkrp(): pl.pallas_call(mttkrp_kernel, out_shape=(jax.ShapeDtypeStruct((rows_i, ra...  5.55 us
    all_to_all x1, starting transfers between devices, local(): parts = lax.all_to_all(parts, 'col', 0, 0)  5.49 us
    pallas_call x1, Pallas kernels, solve(): pl.pallas_call(solve_kernel, out_shape=(jax.ShapeDtypeStruct((packed.shap...  3.22 us
    pallas_call x1, Pallas kernels, first_half(): pl.pallas_call(first_kernel, out_shape=(half, half), compiler_params=pltp...  3.1 us
  transfers between devices with their start and end apart: 5, of which 4 were waited for; matrix products, arithmetic and copies ran while one was open for 0% of the time, Pallas kernels for 10%

profile of v6, /device:TPU:1, one launch (start us, length us, event | category | flops | bytes accessed | tf_op | source)
XLA Modules:
  0.0 85.1 jit_solution(8647316350420400354)
XLA Ops:
  0.6 1.4 %broadcast_in_dim.18 = f32[8,16,256]{2,1,0:T(8,128)} broadcast(f32[16,256]{1,0:T(8,128)} %bitcast.4), dimensions={1,2} | broadcast | bytes 147456 | tf_op jit(solution)/shard_map/broadcast_in_dim | solution.py:351
  2.0 11.6 %all-to-all-start = ((f32[8,16,256]{2,1,0:T(8,128)}), f32[8,16,256]{2,1,0:T(8,128)S(1)}, u32[]{:S(2)}, u32[]{:S(2)}) async-start(f32[8,16,256]{2,1,0:T(8,128)} %broadcast_in_dim.18), calls=%async_computation | async-start | bytes 262144 | tf_op jit(solution)/shard_map/all_to_all | solution.py:352
  13.7 9.3 %all-to-all-done.mine_ref = f32[8,16,256]{2,1,0:T(8,128)S(1)} async-done(((f32[8,16,256]{2,1,0:T(8,128)}), f32[8,16,256]{2,1,0:T(8,128)S(1)}, u32[]{:S(2)}, u32[]{:S(2)}) %all-to-all-start) | async-done | bytes 131104 | tf_op jit(solution)/shard_map/all_to_all | solution.py:352
  23.0 2.1 %collective-permute-start = (f32[8,16,256]{2,1,0:T(8,128)S(1)}, f32[8,16,256]{2,1,0:T(8,128)S(1)}, u32[]{:S(2)}, u32[]{:S(2)}) collective-permute-start(f32[8,16,256]{2,1,0:T(8,128)S(1)} %all-to-all-done.mine_ref), channel_id=1, source_target_pairs={{0,16},{16,0},{32,48},{48,32},{64,80},{80,64},{96,112},{112,96},{1... | collective-permute-start | bytes 393224 | tf_op jit(solution)/shard_map/ppermute | solution.py:353
  25.1 0.3 gram_own.1.own_ref
  25.4 0.0 copy-start
  25.4 0.7 collective-permute-done.other_ref
  26.1 0.9 %gram_part.1 = (f32[256,256]{1,0:T(8,128)S(1)}, f32[16,8,256]{2,1,0:T(8,128)}) custom-call(f32[8,16,256]{2,1,0:T(8,128)S(1)} %all-to-all-done.mine_ref, f32[8,16,256]{2,1,0:T(8,128)S(1)} %collective-permute-done.other_ref, f32[128,128]{1,0:T(8,128)S(1)} %gram_own.1.own_ref), custom_call_target="tpu_custom_call" | custom-call | flops 10000000000 | bytes 524288 | tf_op jit(solution)/shard_map/gram_part/pallas_call | solution.py:59
  27.0 5.5 %all-to-all-start.1 = ((f32[16,8,256]{2,1,0:T(8,128)}), f32[16,8,256]{2,1,0:T(8,128)S(1)}, u32[]{:S(2)}, u32[]{:S(2)}) async-start(f32[16,8,256]{2,1,0:T(8,128)} %get-tuple-element.12), calls=%async_computation.1 | async-start | bytes 262144 | tf_op jit(solution)/shard_map/all_to_all | solution.py:355
  32.5 0.0 copy-done
  32.5 5.5 %mttkrp.1 = (f32[256,256]{1,0:T(8,128)S(1)}, f32[256,256]{1,0:T(8,128)S(1)}) custom-call(s32[1]{0:T(128)} %bitcast.core_ref, f32[32,256,256]{2,1,0:T(8,128)} %slab_hbm.1, f32[256,256]{1,0:T(8,128)S(1)} %get-tuple-element.13.block_ref, f32[32,256]{1,0:T(8,128)S(1)} %copy-done), custom_call_target="tpu_custom_call" | custom-call | flops 3221225472 | bytes 8388608 | tf_op jit(solution)/shard_map/mttkrp/pallas_call | solution.py:131
  38.1 2.2 %all-to-all-done.1.parts_ref = f32[16,8,256]{2,1,0:T(8,128)S(1)} async-done(((f32[16,8,256]{2,1,0:T(8,128)}), f32[16,8,256]{2,1,0:T(8,128)S(1)}, u32[]{:S(2)}, u32[]{:S(2)}) %all-to-all-start.1) | async-done | bytes 131104 | tf_op jit(solution)/shard_map/all_to_all | solution.py:355
  40.3 16.0 %all_to_all.20.packed_ref = f32[16,24,256]{2,1,0:T(8,128)S(1)} all-to-all(f32[16,24,256]{2,1,0:T(8,128)S(1)} %pack.1), channel_id=1, replica_groups=mesh['row'=16,'col'=16] {'col'}, dimensions={0} | all-to-all | bytes 786432 | tf_op jit(solution)/shard_map/all_to_all | solution.py:357
  56.3 2.8 %collective-permute-start.1 = (f32[16,8,256]{2,1,0:T(8,128)S(1)}, f32[16,8,256]{2,1,0:T(8,128)S(1)}, u32[]{:S(2)}, u32[]{:S(2)}) collective-permute-start(f32[16,8,256]{2,1,0:T(8,128)S(1)} %slice.4), channel_id=1, source_target_pairs={{0,16},{16,0},{32,48},{48,32},{64,80},{80,64},{96,112},{112,96},{1... | collective-permute-start | bytes 393224 | tf_op jit(solution)/shard_map/ppermute | solution.py:358
  59.1 3.1 %first_half.1 = (f32[128,256]{1,0:T(8,128)S(1)}, f32[128,256]{1,0:T(8,128)S(1)}) custom-call(f32[16,24,256]{2,1,0:T(8,128)S(1)} %all_to_all.20.packed_ref, f32[256,256]{1,0:T(8,128)S(1)} %get-tuple-element.15.gram_c_ref), custom_call_target="tpu_custom_call" | custom-call | flops 10000000000 | bytes 393216 | tf_op jit(solution)/shard_map/first_half/pallas_call | solution.py:279
  62.2 0.0 collective-permute-done.1.other_ref
  62.2 3.2 %solve.1 = (f32[16,256]{1,0:T(8,128)S(1)}, f32[1,256]{1,0:T(1,128)S(1)}) custom-call(s32[1]{0:T(128)} %bitcast.core_ref, f32[128,256]{1,0:T(8,128)S(1)} %get-tuple-element.16.own_ref, f32[128,256]{1,0:T(8,128)S(1)} %get-tuple-element.17.change_ref, f32[16,24,256]{2,1,0:T(8,128)S(1)} %all_to_all.20.packed_ref, ...), custom_call_target="tpu_custom_call" | custom-call | tf_op jit(solution)/shard_map/solve/pallas_call | solution.py:309
  65.5 0.1 collective-permute-start.2
  65.6 1.1 %collective-permute-done.2 = f32[1,256]{1,0:T(1,128)S(1)} collective-permute-done((f32[1,256]{1,0:T(1,128)S(1)}, f32[1,256]{1,0:T(1,128)S(1)}, u32[]{:S(2)}, u32[]{:S(2)}) %collective-permute-start.2) | collective-permute-done | bytes 1056 | tf_op jit(solution)/shard_map/ppermute | solution.py:361
  66.7 0.1 broadcast_in_dim.20
  66.8 17.6 %all_to_all.21.squares_ref = f32[128,1,256]{2,1,0:T(1,128)S(1)} all-to-all(f32[128,1,256]{2,1,0:T(1,128)S(1)} %broadcast_in_dim.20), channel_id=1, replica_groups={{0,1,2,3,4,5,6,7,8,9,10,11,12,13,14,15,32,33,34,35,36,37,38,39,40,41,42..., dimensions={0} | all-to-all | bytes 262144 | tf_op jit(solution)/shard_map/all_to_all | solution.py:367
  84.4 0.8 finish.1
  (3 shorter events, 0.0 us)
Async XLA Ops:
  2.0 21.0 %all-to-all-start = ((f32[8,16,256]{2,1,0:T(8,128)}), f32[8,16,256]{2,1,0:T(8,128)S(1)}, u32[]{:S(2)}, u32[]{:S(2)}) async-start(f32[8,16,256]{2,1,0:T(8,128)} %broadcast_in_dim.18), calls=%async_computation | async-start | bytes 262144 | tf_op jit(solution)/shard_map/all_to_all | solution.py:352
  23.0 3.1 %collective-permute-start = (f32[8,16,256]{2,1,0:T(8,128)S(1)}, f32[8,16,256]{2,1,0:T(8,128)S(1)}, u32[]{:S(2)}, u32[]{:S(2)}) collective-permute-start(f32[8,16,256]{2,1,0:T(8,128)S(1)} %all-to-all-done.mine_ref), channel_id=1, source_target_pairs={{0,16},{16,0},{32,48},{48,32},{64,80},{80,64},{96,112},{112,96},{1... | collective-permute-start | bytes 393224 | tf_op jit(solution)/shard_map/ppermute | solution.py:353
  25.4 7.1 %copy-start = (f32[32,256]{1,0:T(8,128)S(1)}, f32[32,256]{1,0:T(8,128)}, u32[]{:S(2)}) copy-start(f32[32,256]{1,0:T(8,128)} %c_ref.1) | copy-start | bytes 98308
  27.0 13.3 %all-to-all-start.1 = ((f32[16,8,256]{2,1,0:T(8,128)}), f32[16,8,256]{2,1,0:T(8,128)S(1)}, u32[]{:S(2)}, u32[]{:S(2)}) async-start(f32[16,8,256]{2,1,0:T(8,128)} %get-tuple-element.12), calls=%async_computation.1 | async-start | bytes 262144 | tf_op jit(solution)/shard_map/all_to_all | solution.py:355
  56.3 5.9 %collective-permute-start.1 = (f32[16,8,256]{2,1,0:T(8,128)S(1)}, f32[16,8,256]{2,1,0:T(8,128)S(1)}, u32[]{:S(2)}, u32[]{:S(2)}) collective-permute-start(f32[16,8,256]{2,1,0:T(8,128)S(1)} %slice.4), channel_id=1, source_target_pairs={{0,16},{16,0},{32,48},{48,32},{64,80},{80,64},{96,112},{112,96},{1... | collective-permute-start | bytes 393224 | tf_op jit(solution)/shard_map/ppermute | solution.py:358
  65.5 1.2 %collective-permute-start.2 = (f32[1,256]{1,0:T(1,128)S(1)}, f32[1,256]{1,0:T(1,128)S(1)}, u32[]{:S(2)}, u32[]{:S(2)}) collective-permute-start(f32[1,256]{1,0:T(1,128)S(1)} %get-tuple-element.18), channel_id=1, source_target_pairs={{0,16},{16,0},{32,48},{48,32},{64,80},{80,64},{96,112},{112,96},{1... | collective-permute-start | bytes 3080 | tf_op jit(solution)/shard_map/ppermute | solution.py:361

commit v7 on v5

--- a/solution.py
+++ b/solution.py
@@ -179,16 +179,20 @@
     unit = jnp.where(lane == row, 1.0, 0.0)
     tiles[tile] = jnp.where((lane >= 0) & (lane < pivots), unit, tiles[tile])
     scale = jnp.ones(shape, f32)
+    pivot = over_rows(cols[0], 0)
     for q in range(pivots):
         here = row == q
+        inverse = 1.0 / pivot
+        near = range(q + 1, min(q + 1 + 1, pivots))
+        masked = jnp.where(here, 0.0, cols[q])
+        change = [masked * over_rows(cols[p], q) for p in near]
         if q + 1 < pivots:
-            change = jnp.where(here, 0.0, cols[q] * over_rows(cols[q + 1], q))
-        inverse = jnp.broadcast_to(1.0 / cols[q][q : q + 1], shape)
-        factor = jnp.where(here, 0.0, cols[q] * inverse)
+            pivot = over_rows(cols[q + 1], q + 1) - over_rows(change[0], q + 1) * inverse
+        factor = masked * inverse
         scale = jnp.where(here, inverse, scale)
-        if q + 1 < pivots:
-            cols[q + 1] = cols[q + 1] - change * inverse
-        for p in range(q + 2, pivots):
+        for p, term in zip(near, change):
+            cols[p] = cols[p] - term * inverse
+        for p in range(q + 1 + 1, pivots):
             cols[p] = cols[p] - factor * over_rows(cols[p], q)
         tiles = [part - factor * over_rows(part, q) for part in tiles]
     return [part * scale for part in tiles]
@@ -330,13 +334,23 @@
     other = lax.ppermute(packed[:, : parts.shape[1]], "row", swap)
     own, change = first_half(packed, gram_c)
     solved, squares = solve(core, own, change, packed, other, gram_c)
-    squares = squares + lax.ppermute(squares, "row", swap)
-    same_core = [
-        [(2 * chip + core) * n_col + c for chip in range(chips) for c in range(n_col)]
-        for core in range(2)
+    beside_x = [(i, i ^ 1) for i in range(n_col)]
+    across = [((i * n_col) + j, (i ^ 1) * n_col + (j ^ 1)) for i in range(n_row) for j in range(n_col)]
+    chip = squares + lax.ppermute(squares, "row", swap)
+    neighbour = lax.ppermute(squares, "col", beside_x) + lax.ppermute(squares, both, across)
+    squares = chip + neighbour
+    group = [
+        [
+            (2 * pair + which) * n_col + c
+            for pair in range(chips)
+            for c in range(n_col)
+            if c % 4 in ends
+        ]
+        for which in range(2)
+        for ends in ((0, 3), (1, 2))
     ]
-    copies = jnp.broadcast_to(squares[None], (chips * n_col,) + squares.shape)
-    squares = lax.all_to_all(copies, both, 0, 0, axis_index_groups=same_core)
+    copies = jnp.broadcast_to(squares[None], (len(group[0]),) + squares.shape)
+    squares = lax.all_to_all(copies, both, 0, 0, axis_index_groups=group)
     factor_a, col_scale = finish(squares, solved, rows_i * n_row)
     return (factor_a, col_scale[0])
 

time: 84.8 us -> 84.9 us (level)
  starting transfers between devices: 10.5 us -> 12.6 us
  blocking collectives: 54.3 us -> 52.2 us
    all_to_all x1, blocking collectives: 17.6 us -> 15.4 us  [local(): squares = lax.all_to_all(copies, both, 0, 0, axis_index_groups=group)]
    ppermute x1 -> x3, starting transfers between devices: 0.1 us -> 2.22 us  [the longest x1 1.35 us: local(): lax.ppermute(squares, 'col', beside_x) + lax.ppermute(squares, both, across)]
  transfers between devices with their start and end apart: 4 -> 6, of which waited for: 3 -> 3; matrix products, arithmetic and copies ran while one was open for 0% -> 0% of each run, Pallas kernels for 10% -> 10%
where the time goes in v7:
time: 84.9 us; the launch traced here: 84 us
  blocking collectives  52.2 us (61%)
  Pallas kernels  13.7 us (16%)
  starting transfers between devices  12.6 us (15%)
  waiting for transfers between devices  4.06 us (5%)
    all_to_all x1, blocking collectives, local(): mine = lax.all_to_all(copies, 'row', 0, 0, axis_index_groups=same_core)  20.8 us
    all_to_all x1, blocking collectives, local(): packed = lax.all_to_all(pack(parts, terms), 'col', 0, 0)  16 us
    all_to_all x1, blocking collectives, local(): squares = lax.all_to_all(copies, both, 0, 0, axis_index_groups=group)  15.4 us
    pallas_call x1, Pallas kernels, mttkrp(): pl.pallas_call(mttkrp_kernel, out_shape=(jax.ShapeDtypeStruct((rows_i, ra...  5.54 us
    all_to_all x1, starting transfers between devices, local(): parts = lax.all_to_all(parts, 'col', 0, 0)  5.49 us
    pallas_call x1, Pallas kernels, solve(): pl.pallas_call(solve_kernel, out_shape=(jax.ShapeDtypeStruct((packed.shap...  3.22 us
    pallas_call x1, Pallas kernels, first_half(): pl.pallas_call(first_kernel, out_shape=(half, half), compiler_params=pltp...  3.1 us
    ppermute x1, starting transfers between devices, local(): other = lax.ppermute(packed[:, :parts.shape[1]], 'row', swap)  2.82 us
  transfers between devices with their start and end apart: 6, of which 3 were waited for; matrix products, arithmetic and copies ran while one was open for 0% of the time, Pallas kernels for 10%

profile of v7, /device:TPU:1, one launch (start us, length us, event | category | flops | bytes accessed | tf_op | source)
XLA Modules:
  0.0 84.0 jit_solution(9597086544949757054)
XLA Ops:
  0.6 0.7 broadcast_in_dim.18
  1.4 20.8 %all_to_all.20.mine_ref = f32[8,16,256]{2,1,0:T(8,128)S(1)} all-to-all(f32[8,16,256]{2,1,0:T(8,128)S(1)} %broadcast_in_dim.18), channel_id=1, replica_groups={{0,32,64,96,128,160,192,224},{16,48,80,112,144,176,208,240},{1,33,65,97..., dimensions={0} | all-to-all | bytes 262144 | tf_op jit(solution)/shard_map/all_to_all | solution.py:328
  22.1 2.1 %collective-permute-start = (f32[8,16,256]{2,1,0:T(8,128)S(1)}, f32[8,16,256]{2,1,0:T(8,128)S(1)}, u32[]{:S(2)}, u32[]{:S(2)}) collective-permute-start(f32[8,16,256]{2,1,0:T(8,128)S(1)} %all_to_all.20.mine_ref), channel_id=1, source_target_pairs={{0,16},{16,0},{32,48},{48,32},{64,80},{80,64},{96,112},{112,96},{1... | collective-permute-start | bytes 393224 | tf_op jit(solution)/shard_map/ppermute | solution.py:329
  24.2 0.0 copy-start
  24.2 1.0 %collective-permute-done.other_ref = f32[8,16,256]{2,1,0:T(8,128)S(1)} collective-permute-done((f32[8,16,256]{2,1,0:T(8,128)S(1)}, f32[8,16,256]{2,1,0:T(8,128)S(1)}, u32[]{:S(2)}, u32[]{:S(2)}) %collective-permute-start) | collective-permute-done | bytes 131104 | tf_op jit(solution)/shard_map/ppermute | solution.py:329
  25.2 1.1 %gram_part.1 = (f32[256,256]{1,0:T(8,128)S(1)}, f32[16,8,256]{2,1,0:T(8,128)}) custom-call(f32[8,16,256]{2,1,0:T(8,128)S(1)} %all_to_all.20.mine_ref, f32[8,16,256]{2,1,0:T(8,128)S(1)} %collective-permute-done.other_ref), custom_call_target="tpu_custom_call" | custom-call | flops 10000000000 | bytes 524288 | tf_op jit(solution)/shard_map/gram_part/pallas_call | solution.py:35
  26.3 5.5 %all-to-all-start.1 = ((f32[16,8,256]{2,1,0:T(8,128)}), f32[16,8,256]{2,1,0:T(8,128)S(1)}, u32[]{:S(2)}, u32[]{:S(2)}) async-start(f32[16,8,256]{2,1,0:T(8,128)} %get-tuple-element.12), calls=%async_computation.1 | async-start | bytes 262144 | tf_op jit(solution)/shard_map/all_to_all | solution.py:331
  31.8 0.0 copy-done
  31.8 5.5 %mttkrp.1 = (f32[256,256]{1,0:T(8,128)S(1)}, f32[256,256]{1,0:T(8,128)S(1)}) custom-call(s32[1]{0:T(128)} %bitcast.core_ref, f32[32,256,256]{2,1,0:T(8,128)} %slab_hbm.1, f32[256,256]{1,0:T(8,128)S(1)} %get-tuple-element.13.block_ref, f32[32,256]{1,0:T(8,128)S(1)} %copy-done), custom_call_target="tpu_custom_call" | custom-call | flops 3221225472 | bytes 8388608 | tf_op jit(solution)/shard_map/mttkrp/pallas_call | solution.py:107
  37.4 2.2 %all-to-all-done.1.parts_ref = f32[16,8,256]{2,1,0:T(8,128)S(1)} async-done(((f32[16,8,256]{2,1,0:T(8,128)}), f32[16,8,256]{2,1,0:T(8,128)S(1)}, u32[]{:S(2)}, u32[]{:S(2)}) %all-to-all-start.1) | async-done | bytes 131104 | tf_op jit(solution)/shard_map/all_to_all | solution.py:331
  39.6 16.0 %all_to_all.21.packed_ref = f32[16,24,256]{2,1,0:T(8,128)S(1)} all-to-all(f32[16,24,256]{2,1,0:T(8,128)S(1)} %pack.1), channel_id=1, replica_groups=mesh['row'=16,'col'=16] {'col'}, dimensions={0} | all-to-all | bytes 786432 | tf_op jit(solution)/shard_map/all_to_all | solution.py:333
  55.6 2.8 %collective-permute-start.1 = (f32[16,8,256]{2,1,0:T(8,128)S(1)}, f32[16,8,256]{2,1,0:T(8,128)S(1)}, u32[]{:S(2)}, u32[]{:S(2)}) collective-permute-start(f32[16,8,256]{2,1,0:T(8,128)S(1)} %slice.4), channel_id=1, source_target_pairs={{0,16},{16,0},{32,48},{48,32},{64,80},{80,64},{96,112},{112,96},{1... | collective-permute-start | bytes 393224 | tf_op jit(solution)/shard_map/ppermute | solution.py:334
  58.4 3.1 %first_half.1 = (f32[128,256]{1,0:T(8,128)S(1)}, f32[128,256]{1,0:T(8,128)S(1)}) custom-call(f32[16,24,256]{2,1,0:T(8,128)S(1)} %all_to_all.21.packed_ref, f32[256,256]{1,0:T(8,128)S(1)} %get-tuple-element.15.gram_c_ref), custom_call_target="tpu_custom_call" | custom-call | flops 10000000000 | bytes 393216 | tf_op jit(solution)/shard_map/first_half/pallas_call | solution.py:255
  61.5 0.0 collective-permute-done.1.other_ref
  61.5 3.2 %solve.1 = (f32[16,256]{1,0:T(8,128)S(1)}, f32[1,256]{1,0:T(1,128)S(1)}) custom-call(s32[1]{0:T(128)} %bitcast.core_ref, f32[128,256]{1,0:T(8,128)S(1)} %get-tuple-element.16.own_ref, f32[128,256]{1,0:T(8,128)S(1)} %get-tuple-element.17.change_ref, f32[16,24,256]{2,1,0:T(8,128)S(1)} %all_to_all.21.packed_ref, ...), custom_call_target="tpu_custom_call" | custom-call | tf_op jit(solution)/shard_map/solve/pallas_call | solution.py:285
  64.8 0.1 collective-permute-start.4
  64.9 1.4 %collective-permute-start.3 = (f32[1,256]{1,0:T(1,128)S(1)}, f32[1,256]{1,0:T(1,128)S(1)}, u32[]{:S(2)}, u32[]{:S(2)}) collective-permute-start(f32[1,256]{1,0:T(1,128)S(1)} %get-tuple-element.18), channel_id=1, source_target_pairs={{0,1},{1,0},{2,3},{3,2},{4,5},{5,4},{6,7},{7,6},{8,9},{9,8},{10,11... | collective-permute-start | bytes 3080 | tf_op jit(solution)/shard_map/ppermute | solution.py:340
  66.2 0.8 collective-permute-start.2
  67.0 0.9 %collective-permute-done.4 = f32[1,256]{1,0:T(1,128)S(1)} collective-permute-done((f32[1,256]{1,0:T(1,128)S(1)}, f32[1,256]{1,0:T(1,128)S(1)}, u32[]{:S(2)}, u32[]{:S(2)}) %collective-permute-start.4) | collective-permute-done | bytes 1056 | tf_op jit(solution)/shard_map/ppermute | solution.py:340
  67.8 0.0 collective-permute-done.3
  67.8 0.0 collective-permute-done.2
  67.9 15.4 %all_to_all.22.squares_ref = f32[64,1,256]{2,1,0:T(1,128)S(1)} all-to-all(f32[64,1,256]{2,1,0:T(1,128)S(1)} %broadcast_in_dim.20), channel_id=1, replica_groups={{0,3,4,7,8,11,12,15,32,35,36,39,40,43,44,47,64,67,68,71,72,75,76,79,96,..., dimensions={0} | all-to-all | bytes 131072 | tf_op jit(solution)/shard_map/all_to_all | solution.py:353
  83.3 0.7 finish.1
  (4 shorter events, 0.1 us)
Async XLA Ops:
  22.1 3.1 %collective-permute-start = (f32[8,16,256]{2,1,0:T(8,128)S(1)}, f32[8,16,256]{2,1,0:T(8,128)S(1)}, u32[]{:S(2)}, u32[]{:S(2)}) collective-permute-start(f32[8,16,256]{2,1,0:T(8,128)S(1)} %all_to_all.20.mine_ref), channel_id=1, source_target_pairs={{0,16},{16,0},{32,48},{48,32},{64,80},{80,64},{96,112},{112,96},{1... | collective-permute-start | bytes 393224 | tf_op jit(solution)/shard_map/ppermute | solution.py:329
  24.2 7.6 %copy-start = (f32[32,256]{1,0:T(8,128)S(1)}, f32[32,256]{1,0:T(8,128)}, u32[]{:S(2)}) copy-start(f32[32,256]{1,0:T(8,128)} %c_ref.1) | copy-start | bytes 98308
  26.3 13.3 %all-to-all-start.1 = ((f32[16,8,256]{2,1,0:T(8,128)}), f32[16,8,256]{2,1,0:T(8,128)S(1)}, u32[]{:S(2)}, u32[]{:S(2)}) async-start(f32[16,8,256]{2,1,0:T(8,128)} %get-tuple-element.12), calls=%async_computation.1 | async-start | bytes 262144 | tf_op jit(solution)/shard_map/all_to_all | solution.py:331
  55.6 5.9 %collective-permute-start.1 = (f32[16,8,256]{2,1,0:T(8,128)S(1)}, f32[16,8,256]{2,1,0:T(8,128)S(1)}, u32[]{:S(2)}, u32[]{:S(2)}) collective-permute-start(f32[16,8,256]{2,1,0:T(8,128)S(1)} %slice.4), channel_id=1, source_target_pairs={{0,16},{16,0},{32,48},{48,32},{64,80},{80,64},{96,112},{112,96},{1... | collective-permute-start | bytes 393224 | tf_op jit(solution)/shard_map/ppermute | solution.py:334
  64.8 3.1 %collective-permute-start.4 = (f32[1,256]{1,0:T(1,128)S(1)}, f32[1,256]{1,0:T(1,128)S(1)}, u32[]{:S(2)}, u32[]{:S(2)}) collective-permute-start(f32[1,256]{1,0:T(1,128)S(1)} %get-tuple-element.18), channel_id=1, source_target_pairs={{0,17},{1,16},{2,19},{3,18},{4,21},{5,20},{6,23},{7,22},{8,25},{9,... | collective-permute-start | bytes 3080 | tf_op jit(solution)/shard_map/ppermute | solution.py:340
  64.9 3.0 %collective-permute-start.3 = (f32[1,256]{1,0:T(1,128)S(1)}, f32[1,256]{1,0:T(1,128)S(1)}, u32[]{:S(2)}, u32[]{:S(2)}) collective-permute-start(f32[1,256]{1,0:T(1,128)S(1)} %get-tuple-element.18), channel_id=1, source_target_pairs={{0,1},{1,0},{2,3},{3,2},{4,5},{5,4},{6,7},{7,6},{8,9},{9,8},{10,11... | collective-permute-start | bytes 3080 | tf_op jit(solution)/shard_map/ppermute | solution.py:340
  66.2 1.6 %collective-permute-start.2 = (f32[1,256]{1,0:T(1,128)S(1)}, f32[1,256]{1,0:T(1,128)S(1)}, u32[]{:S(2)}, u32[]{:S(2)}) collective-permute-start(f32[1,256]{1,0:T(1,128)S(1)} %get-tuple-element.18), channel_id=1, source_target_pairs={{0,16},{16,0},{32,48},{48,32},{64,80},{80,64},{96,112},{112,96},{1... | collective-permute-start | bytes 3080 | tf_op jit(solution)/shard_map/ppermute | solution.py:339

commit v8 on v5

--- a/solution.py
+++ b/solution.py
@@ -25,7 +25,9 @@
     mine = mine_ref[...].reshape(part_ref.shape[0] * part_ref.shape[1], block_ref.shape[1])
     block_ref[: mine.shape[0]] = mine
     block_ref[mine.shape[0] :] = other_ref[...].reshape(mine.shape)
-    part = lax.dot_general(mine, block_ref[...], nt, precision=high, preferred_element_type=f32)
+    part = lax.dot_general(
+        left_parts(mine, 1), right_parts(block_ref[...], 1), nt, preferred_element_type=f32
+    )
     part_ref[...] = part.reshape(part_ref.shape)
 
 
@@ -150,14 +152,14 @@
     return top, middle, (rest - middle.astype(f32)).astype(bf16)
 
 
-def left_parts(value):
+def left_parts(value, axis=0):
     top, middle, low = split(value)
-    return jnp.concatenate([top, top, middle, top, middle, low], axis=0)
-
-
-def right_parts(value):
+    return jnp.concatenate([top, top, middle, top, middle, low], axis=axis)
+
+
+def right_parts(value, axis=0):
     top, middle, low = split(value)
-    return jnp.concatenate([top, middle, top, low, middle, top], axis=0)
+    return jnp.concatenate([top, middle, top, low, middle, top], axis=axis)
 
 
 def spread(block, offset):
@@ -270,7 +272,9 @@
     gram_ref[half:, half:] = other - change_ref[:, half:]
     invert(gram_ref, half, ranks)
     mine = jnp.sum(packed_ref[:, rows:], axis=0)
-    solved = jnp.dot(mine, gram_ref[...], precision=high, preferred_element_type=f32)
+    solved = jnp.dot(
+        left_parts(mine, 1), right_parts(gram_ref[...]), preferred_element_type=f32
+    )
     solved = by_turns(core_ref[0], solved)
     solved_ref[...] = solved
     squares_ref[...] = jnp.sum(solved * solved, axis=0, keepdims=True)

time: 84.8 us -> 84.8 us (level)
  no operation moved by 1% of the time
where the time goes in v8:
time: 84.8 us; the launch traced here: 84.4 us
  blocking collectives  54.3 us (64%)
  Pallas kernels  13.8 us (16%)
  starting transfers between devices  10.5 us (12%)
  waiting for transfers between devices  4.33 us (5%)
    all_to_all x1, blocking collectives, local(): mine = lax.all_to_all(copies, 'row', 0, 0, axis_index_groups=same_core)  20.8 us
    all_to_all x1, blocking collectives, local(): squares = lax.all_to_all(copies, both, 0, 0, axis_index_groups=same_core)  17.6 us
    all_to_all x1, blocking collectives, local(): packed = lax.all_to_all(pack(parts, terms), 'col', 0, 0)  16 us
    pallas_call x1, Pallas kernels, mttkrp(): pl.pallas_call(mttkrp_kernel, out_shape=(jax.ShapeDtypeStruct((rows_i, ra...  5.54 us
    all_to_all x1, starting transfers between devices, local(): parts = lax.all_to_all(parts, 'col', 0, 0)  5.49 us
    pallas_call x1, Pallas kernels, solve(): pl.pallas_call(solve_kernel, out_shape=(jax.ShapeDtypeStruct((packed.shap...  3.28 us
    pallas_call x1, Pallas kernels, first_half(): pl.pallas_call(first_kernel, out_shape=(half, half), compiler_params=pltp...  3.08 us
    ppermute x1, starting transfers between devices, local(): other = lax.ppermute(packed[:, :parts.shape[1]], 'row', swap)  2.82 us
  transfers between devices with their start and end apart: 4, of which 3 were waited for; matrix products, arithmetic and copies ran while one was open for 0% of the time, Pallas kernels for 10%

profile of v8, /device:TPU:1, one launch (start us, length us, event | category | flops | bytes accessed | tf_op | source)
XLA Modules:
  0.0 84.4 jit_solution(15651948048125575093)
XLA Ops:
  0.6 0.7 broadcast_in_dim.18
  1.4 20.8 %all_to_all.20.mine_ref = f32[8,16,256]{2,1,0:T(8,128)S(1)} all-to-all(f32[8,16,256]{2,1,0:T(8,128)S(1)} %broadcast_in_dim.18), channel_id=1, replica_groups={{0,32,64,96,128,160,192,224},{16,48,80,112,144,176,208,240},{1,33,65,97..., dimensions={0} | all-to-all | bytes 262144 | tf_op jit(solution)/shard_map/all_to_all | solution.py:328
  22.1 2.1 %collective-permute-start = (f32[8,16,256]{2,1,0:T(8,128)S(1)}, f32[8,16,256]{2,1,0:T(8,128)S(1)}, u32[]{:S(2)}, u32[]{:S(2)}) collective-permute-start(f32[8,16,256]{2,1,0:T(8,128)S(1)} %all_to_all.20.mine_ref), channel_id=1, source_target_pairs={{0,16},{16,0},{32,48},{48,32},{64,80},{80,64},{96,112},{112,96},{1... | collective-permute-start | bytes 393224 | tf_op jit(solution)/shard_map/ppermute | solution.py:329
  24.2 0.0 copy-start
  24.2 1.0 %collective-permute-done.other_ref = f32[8,16,256]{2,1,0:T(8,128)S(1)} collective-permute-done((f32[8,16,256]{2,1,0:T(8,128)S(1)}, f32[8,16,256]{2,1,0:T(8,128)S(1)}, u32[]{:S(2)}, u32[]{:S(2)}) %collective-permute-start) | collective-permute-done | bytes 131104 | tf_op jit(solution)/shard_map/ppermute | solution.py:329
  25.2 1.1 %gram_part.1 = (f32[256,256]{1,0:T(8,128)S(1)}, f32[16,8,256]{2,1,0:T(8,128)}) custom-call(f32[8,16,256]{2,1,0:T(8,128)S(1)} %all_to_all.20.mine_ref, f32[8,16,256]{2,1,0:T(8,128)S(1)} %collective-permute-done.other_ref), custom_call_target="tpu_custom_call" | custom-call | flops 10000000000 | bytes 524288 | tf_op jit(solution)/shard_map/gram_part/pallas_call | solution.py:37
  26.3 5.5 %all-to-all-start.1 = ((f32[16,8,256]{2,1,0:T(8,128)}), f32[16,8,256]{2,1,0:T(8,128)S(1)}, u32[]{:S(2)}, u32[]{:S(2)}) async-start(f32[16,8,256]{2,1,0:T(8,128)} %get-tuple-element.12), calls=%async_computation.1 | async-start | bytes 262144 | tf_op jit(solution)/shard_map/all_to_all | solution.py:331
  31.8 0.0 copy-done
  31.8 5.5 %mttkrp.1 = (f32[256,256]{1,0:T(8,128)S(1)}, f32[256,256]{1,0:T(8,128)S(1)}) custom-call(s32[1]{0:T(128)} %bitcast.core_ref, f32[32,256,256]{2,1,0:T(8,128)} %slab_hbm.1, f32[256,256]{1,0:T(8,128)S(1)} %get-tuple-element.13.block_ref, f32[32,256]{1,0:T(8,128)S(1)} %copy-done), custom_call_target="tpu_custom_call" | custom-call | flops 3221225472 | bytes 8388608 | tf_op jit(solution)/shard_map/mttkrp/pallas_call | solution.py:109
  37.3 2.2 %all-to-all-done.1.parts_ref = f32[16,8,256]{2,1,0:T(8,128)S(1)} async-done(((f32[16,8,256]{2,1,0:T(8,128)}), f32[16,8,256]{2,1,0:T(8,128)S(1)}, u32[]{:S(2)}, u32[]{:S(2)}) %all-to-all-start.1) | async-done | bytes 131104 | tf_op jit(solution)/shard_map/all_to_all | solution.py:331
  39.6 16.0 %all_to_all.21.packed_ref = f32[16,24,256]{2,1,0:T(8,128)S(1)} all-to-all(f32[16,24,256]{2,1,0:T(8,128)S(1)} %pack.1), channel_id=1, replica_groups=mesh['row'=16,'col'=16] {'col'}, dimensions={0} | all-to-all | bytes 786432 | tf_op jit(solution)/shard_map/all_to_all | solution.py:333
  55.6 2.8 %collective-permute-start.1 = (f32[16,8,256]{2,1,0:T(8,128)S(1)}, f32[16,8,256]{2,1,0:T(8,128)S(1)}, u32[]{:S(2)}, u32[]{:S(2)}) collective-permute-start(f32[16,8,256]{2,1,0:T(8,128)S(1)} %slice.4), channel_id=1, source_target_pairs={{0,16},{16,0},{32,48},{48,32},{64,80},{80,64},{96,112},{112,96},{1... | collective-permute-start | bytes 393224 | tf_op jit(solution)/shard_map/ppermute | solution.py:334
  58.4 3.1 %first_half.1 = (f32[128,256]{1,0:T(8,128)S(1)}, f32[128,256]{1,0:T(8,128)S(1)}) custom-call(f32[16,24,256]{2,1,0:T(8,128)S(1)} %all_to_all.21.packed_ref, f32[256,256]{1,0:T(8,128)S(1)} %get-tuple-element.15.gram_c_ref), custom_call_target="tpu_custom_call" | custom-call | flops 10000000000 | bytes 393216 | tf_op jit(solution)/shard_map/first_half/pallas_call | solution.py:253
  61.5 0.0 collective-permute-done.1.other_ref
  61.5 3.3 %solve.1 = (f32[16,256]{1,0:T(8,128)S(1)}, f32[1,256]{1,0:T(1,128)S(1)}) custom-call(s32[1]{0:T(128)} %bitcast.core_ref, f32[128,256]{1,0:T(8,128)S(1)} %get-tuple-element.16.own_ref, f32[128,256]{1,0:T(8,128)S(1)} %get-tuple-element.17.change_ref, f32[16,24,256]{2,1,0:T(8,128)S(1)} %all_to_all.21.packed_ref, ...), custom_call_target="tpu_custom_call" | custom-call | tf_op jit(solution)/shard_map/solve/pallas_call | solution.py:285
  64.8 0.1 collective-permute-start.2
  64.9 1.1 %collective-permute-done.2 = f32[1,256]{1,0:T(1,128)S(1)} collective-permute-done((f32[1,256]{1,0:T(1,128)S(1)}, f32[1,256]{1,0:T(1,128)S(1)}, u32[]{:S(2)}, u32[]{:S(2)}) %collective-permute-start.2) | collective-permute-done | bytes 1056 | tf_op jit(solution)/shard_map/ppermute | solution.py:337
  66.0 0.1 broadcast_in_dim.20
  66.1 17.6 %all_to_all.22.squares_ref = f32[128,1,256]{2,1,0:T(1,128)S(1)} all-to-all(f32[128,1,256]{2,1,0:T(1,128)S(1)} %broadcast_in_dim.20), channel_id=1, replica_groups={{0,1,2,3,4,5,6,7,8,9,10,11,12,13,14,15,32,33,34,35,36,37,38,39,40,41,42..., dimensions={0} | all-to-all | bytes 262144 | tf_op jit(solution)/shard_map/all_to_all | solution.py:343
  83.7 0.8 finish.1
  (3 shorter events, 0.0 us)
Async XLA Ops:
  22.1 3.1 %collective-permute-start = (f32[8,16,256]{2,1,0:T(8,128)S(1)}, f32[8,16,256]{2,1,0:T(8,128)S(1)}, u32[]{:S(2)}, u32[]{:S(2)}) collective-permute-start(f32[8,16,256]{2,1,0:T(8,128)S(1)} %all_to_all.20.mine_ref), channel_id=1, source_target_pairs={{0,16},{16,0},{32,48},{48,32},{64,80},{80,64},{96,112},{112,96},{1... | collective-permute-start | bytes 393224 | tf_op jit(solution)/shard_map/ppermute | solution.py:329
  24.2 7.5 %copy-start = (f32[32,256]{1,0:T(8,128)S(1)}, f32[32,256]{1,0:T(8,128)}, u32[]{:S(2)}) copy-start(f32[32,256]{1,0:T(8,128)} %c_ref.1) | copy-start | bytes 98308
  26.3 13.3 %all-to-all-start.1 = ((f32[16,8,256]{2,1,0:T(8,128)}), f32[16,8,256]{2,1,0:T(8,128)S(1)}, u32[]{:S(2)}, u32[]{:S(2)}) async-start(f32[16,8,256]{2,1,0:T(8,128)} %get-tuple-element.12), calls=%async_computation.1 | async-start | bytes 262144 | tf_op jit(solution)/shard_map/all_to_all | solution.py:331
  55.6 5.9 %collective-permute-start.1 = (f32[16,8,256]{2,1,0:T(8,128)S(1)}, f32[16,8,256]{2,1,0:T(8,128)S(1)}, u32[]{:S(2)}, u32[]{:S(2)}) collective-permute-start(f32[16,8,256]{2,1,0:T(8,128)S(1)} %slice.4), channel_id=1, source_target_pairs={{0,16},{16,0},{32,48},{48,32},{64,80},{80,64},{96,112},{112,96},{1... | collective-permute-start | bytes 393224 | tf_op jit(solution)/shard_map/ppermute | solution.py:334
  64.8 1.2 %collective-permute-start.2 = (f32[1,256]{1,0:T(1,128)S(1)}, f32[1,256]{1,0:T(1,128)S(1)}, u32[]{:S(2)}, u32[]{:S(2)}) collective-permute-start(f32[1,256]{1,0:T(1,128)S(1)} %get-tuple-element.18), channel_id=1, source_target_pairs={{0,16},{16,0},{32,48},{48,32},{64,80},{80,64},{96,112},{112,96},{1... | collective-permute-start | bytes 3080 | tf_op jit(solution)/shard_map/ppermute | solution.py:337

commit v9 on v6

--- a/solution.py
+++ b/solution.py
@@ -36,9 +36,6 @@
         own_kernel,
         out_shape=jax.ShapeDtypeStruct((half, half), f32),
         compiler_params=pltpu.CompilerParams(vmem_limit_bytes=limit),
-        cost_estimate=pl.CostEstimate(
-            flops=beside, bytes_accessed=4 * mine.size, transcendentals=0
-        ),
         name="gram_own",
     )(mine)
 
@@ -203,20 +200,16 @@
     unit = jnp.where(lane == row, 1.0, 0.0)
     tiles[tile] = jnp.where((lane >= 0) & (lane < pivots), unit, tiles[tile])
     scale = jnp.ones(shape, f32)
-    pivot = over_rows(cols[0], 0)
     for q in range(pivots):
         here = row == q
-        inverse = 1.0 / pivot
-        near = range(q + 1, min(q + 1 + 1, pivots))
-        masked = jnp.where(here, 0.0, cols[q])
-        change = [masked * over_rows(cols[p], q) for p in near]
         if q + 1 < pivots:
-            pivot = over_rows(cols[q + 1], q + 1) - over_rows(change[0], q + 1) * inverse
-        factor = masked * inverse
+            change = jnp.where(here, 0.0, cols[q] * over_rows(cols[q + 1], q))
+        inverse = jnp.broadcast_to(1.0 / cols[q][q : q + 1], shape)
+        factor = jnp.where(here, 0.0, cols[q] * inverse)
         scale = jnp.where(here, inverse, scale)
-        for p, term in zip(near, change):
-            cols[p] = cols[p] - term * inverse
-        for p in range(q + 1 + 1, pivots):
+        if q + 1 < pivots:
+            cols[q + 1] = cols[q + 1] - change * inverse
+        for p in range(q + 2, pivots):
             cols[p] = cols[p] - factor * over_rows(cols[p], q)
         tiles = [part - factor * over_rows(part, q) for part in tiles]
     return [part * scale for part in tiles]

time: 85.6 us -> 84.7 us (0.989)
  blocking collectives: 33.5 us -> 54.3 us
  starting transfers between devices: 22.2 us -> 10.5 us
  waiting for transfers between devices: 13.4 us -> 4.04 us
    all_to_all x0 -> x1, blocking collectives: none -> 20.8 us  [local(): mine = lax.all_to_all(copies, 'row', 0, 0, axis_index_groups=same_core)]
    all_to_all x1 -> x0, starting transfers between devices: 11.6 us -> none  [local(): mine = lax.all_to_all(copies, 'row', 0, 0, axis_index_groups=same_core)]
    all_to_all x1 -> x0, waiting for transfers between devices: 9.34 us -> none  [local(): mine = lax.all_to_all(copies, 'row', 0, 0, axis_index_groups=same_core)]
  transfers between devices with their start and end apart: 5 -> 4, of which waited for: 4 -> 3; matrix products, arithmetic and copies ran while one was open for 0% -> 0% of each run, Pallas kernels for 10% -> 11%
where the time goes in v9:
time: 84.7 us; the launch traced here: 84.3 us
  blocking collectives  54.3 us (64%)
  Pallas kernels  13.9 us (16%)
  starting transfers between devices  10.5 us (12%)
  waiting for transfers between devices  4.04 us (5%)
    all_to_all x1, blocking collectives, local(): mine = lax.all_to_all(copies, 'row', 0, 0, axis_index_groups=same_core)  20.8 us
    all_to_all x1, blocking collectives, local(): squares = lax.all_to_all(copies, both, 0, 0, axis_index_groups=same_core)  17.6 us
    all_to_all x1, blocking collectives, local(): packed = lax.all_to_all(pack(parts, terms), 'col', 0, 0)  16 us
    pallas_call x1, Pallas kernels, mttkrp(): pl.pallas_call(mttkrp_kernel, out_shape=(jax.ShapeDtypeStruct((rows_i, ra...  5.54 us
    all_to_all x1, starting transfers between devices, local(): parts = lax.all_to_all(parts, 'col', 0, 0)  5.49 us
    pallas_call x1, Pallas kernels, solve(): pl.pallas_call(solve_kernel, out_shape=(jax.ShapeDtypeStruct((packed.shap...  3.29 us
    pallas_call x1, Pallas kernels, first_half(): pl.pallas_call(first_kernel, out_shape=(half, half), compiler_params=pltp...  3.08 us
    ppermute x1, starting transfers between devices, local(): other = lax.ppermute(packed[:, :parts.shape[1]], 'row', swap)  2.82 us
  transfers between devices with their start and end apart: 4, of which 3 were waited for; matrix products, arithmetic and copies ran while one was open for 0% of the time, Pallas kernels for 11%

profile of v9, /device:TPU:1, one launch (start us, length us, event | category | flops | bytes accessed | tf_op | source)
XLA Modules:
  0.0 84.3 jit_solution(5346094020553416065)
XLA Ops:
  0.6 0.7 broadcast_in_dim.18
  1.4 20.8 %all_to_all.20.mine_ref = f32[8,16,256]{2,1,0:T(8,128)S(1)} all-to-all(f32[8,16,256]{2,1,0:T(8,128)S(1)} %broadcast_in_dim.18), channel_id=1, replica_groups={{0,32,64,96,128,160,192,224},{16,48,80,112,144,176,208,240},{1,33,65,97..., dimensions={0} | all-to-all | bytes 262144 | tf_op jit(solution)/shard_map/all_to_all | solution.py:345
  22.1 2.1 %collective-permute-start = (f32[8,16,256]{2,1,0:T(8,128)S(1)}, f32[8,16,256]{2,1,0:T(8,128)S(1)}, u32[]{:S(2)}, u32[]{:S(2)}) collective-permute-start(f32[8,16,256]{2,1,0:T(8,128)S(1)} %all_to_all.20.mine_ref), channel_id=1, source_target_pairs={{0,16},{16,0},{32,48},{48,32},{64,80},{80,64},{96,112},{112,96},{1... | collective-permute-start | bytes 393224 | tf_op jit(solution)/shard_map/ppermute | solution.py:346
  24.2 0.3 gram_own.1.own_ref
  24.5 0.0 copy-start
  24.5 0.7 collective-permute-done.other_ref
  25.2 0.9 %gram_part.1 = (f32[256,256]{1,0:T(8,128)S(1)}, f32[16,8,256]{2,1,0:T(8,128)}) custom-call(f32[8,16,256]{2,1,0:T(8,128)S(1)} %all_to_all.20.mine_ref, f32[8,16,256]{2,1,0:T(8,128)S(1)} %collective-permute-done.other_ref, f32[128,128]{1,0:T(8,128)S(1)} %gram_own.1.own_ref), custom_call_target="tpu_custom_call" | custom-call | flops 10000000000 | bytes 524288 | tf_op jit(solution)/shard_map/gram_part/pallas_call | solution.py:56
  26.2 5.5 %all-to-all-start.1 = ((f32[16,8,256]{2,1,0:T(8,128)}), f32[16,8,256]{2,1,0:T(8,128)S(1)}, u32[]{:S(2)}, u32[]{:S(2)}) async-start(f32[16,8,256]{2,1,0:T(8,128)} %get-tuple-element.12), calls=%async_computation.1 | async-start | bytes 262144 | tf_op jit(solution)/shard_map/all_to_all | solution.py:348
  31.7 0.0 copy-done
  31.7 5.5 %mttkrp.1 = (f32[256,256]{1,0:T(8,128)S(1)}, f32[256,256]{1,0:T(8,128)S(1)}) custom-call(s32[1]{0:T(128)} %bitcast.core_ref, f32[32,256,256]{2,1,0:T(8,128)} %slab_hbm.1, f32[256,256]{1,0:T(8,128)S(1)} %get-tuple-element.13.block_ref, f32[32,256]{1,0:T(8,128)S(1)} %copy-done), custom_call_target="tpu_custom_call" | custom-call | flops 3221225472 | bytes 8388608 | tf_op jit(solution)/shard_map/mttkrp/pallas_call | solution.py:128
  37.2 2.2 %all-to-all-done.1.parts_ref = f32[16,8,256]{2,1,0:T(8,128)S(1)} async-done(((f32[16,8,256]{2,1,0:T(8,128)}), f32[16,8,256]{2,1,0:T(8,128)S(1)}, u32[]{:S(2)}, u32[]{:S(2)}) %all-to-all-start.1) | async-done | bytes 131104 | tf_op jit(solution)/shard_map/all_to_all | solution.py:348
  39.5 16.0 %all_to_all.21.packed_ref = f32[16,24,256]{2,1,0:T(8,128)S(1)} all-to-all(f32[16,24,256]{2,1,0:T(8,128)S(1)} %pack.1), channel_id=1, replica_groups=mesh['row'=16,'col'=16] {'col'}, dimensions={0} | all-to-all | bytes 786432 | tf_op jit(solution)/shard_map/all_to_all | solution.py:350
  55.5 2.8 %collective-permute-start.1 = (f32[16,8,256]{2,1,0:T(8,128)S(1)}, f32[16,8,256]{2,1,0:T(8,128)S(1)}, u32[]{:S(2)}, u32[]{:S(2)}) collective-permute-start(f32[16,8,256]{2,1,0:T(8,128)S(1)} %slice.4), channel_id=1, source_target_pairs={{0,16},{16,0},{32,48},{48,32},{64,80},{80,64},{96,112},{112,96},{1... | collective-permute-start | bytes 393224 | tf_op jit(solution)/shard_map/ppermute | solution.py:351
  58.3 3.1 %first_half.1 = (f32[128,256]{1,0:T(8,128)S(1)}, f32[128,256]{1,0:T(8,128)S(1)}) custom-call(f32[16,24,256]{2,1,0:T(8,128)S(1)} %all_to_all.21.packed_ref, f32[256,256]{1,0:T(8,128)S(1)} %get-tuple-element.15.gram_c_ref), custom_call_target="tpu_custom_call" | custom-call | flops 10000000000 | bytes 393216 | tf_op jit(solution)/shard_map/first_half/pallas_call | solution.py:272
  61.4 0.0 collective-permute-done.1.other_ref
  61.4 3.3 %solve.1 = (f32[16,256]{1,0:T(8,128)S(1)}, f32[1,256]{1,0:T(1,128)S(1)}) custom-call(s32[1]{0:T(128)} %bitcast.core_ref, f32[128,256]{1,0:T(8,128)S(1)} %get-tuple-element.16.own_ref, f32[128,256]{1,0:T(8,128)S(1)} %get-tuple-element.17.change_ref, f32[16,24,256]{2,1,0:T(8,128)S(1)} %all_to_all.21.packed_ref, ...), custom_call_target="tpu_custom_call" | custom-call | tf_op jit(solution)/shard_map/solve/pallas_call | solution.py:302
  64.7 0.1 collective-permute-start.2
  64.8 1.1 %collective-permute-done.2 = f32[1,256]{1,0:T(1,128)S(1)} collective-permute-done((f32[1,256]{1,0:T(1,128)S(1)}, f32[1,256]{1,0:T(1,128)S(1)}, u32[]{:S(2)}, u32[]{:S(2)}) %collective-permute-start.2) | collective-permute-done | bytes 1056 | tf_op jit(solution)/shard_map/ppermute | solution.py:354
  65.9 0.1 broadcast_in_dim.20
  66.0 17.6 %all_to_all.22.squares_ref = f32[128,1,256]{2,1,0:T(1,128)S(1)} all-to-all(f32[128,1,256]{2,1,0:T(1,128)S(1)} %broadcast_in_dim.20), channel_id=1, replica_groups={{0,1,2,3,4,5,6,7,8,9,10,11,12,13,14,15,32,33,34,35,36,37,38,39,40,41,42..., dimensions={0} | all-to-all | bytes 262144 | tf_op jit(solution)/shard_map/all_to_all | solution.py:360
  83.6 0.8 finish.1
  (3 shorter events, 0.0 us)
Async XLA Ops:
  22.1 3.1 %collective-permute-start = (f32[8,16,256]{2,1,0:T(8,128)S(1)}, f32[8,16,256]{2,1,0:T(8,128)S(1)}, u32[]{:S(2)}, u32[]{:S(2)}) collective-permute-start(f32[8,16,256]{2,1,0:T(8,128)S(1)} %all_to_all.20.mine_ref), channel_id=1, source_target_pairs={{0,16},{16,0},{32,48},{48,32},{64,80},{80,64},{96,112},{112,96},{1... | collective-permute-start | bytes 393224 | tf_op jit(solution)/shard_map/ppermute | solution.py:346
  24.5 7.1 %copy-start = (f32[32,256]{1,0:T(8,128)S(1)}, f32[32,256]{1,0:T(8,128)}, u32[]{:S(2)}) copy-start(f32[32,256]{1,0:T(8,128)} %c_ref.1) | copy-start | bytes 98308
  26.2 13.3 %all-to-all-start.1 = ((f32[16,8,256]{2,1,0:T(8,128)}), f32[16,8,256]{2,1,0:T(8,128)S(1)}, u32[]{:S(2)}, u32[]{:S(2)}) async-start(f32[16,8,256]{2,1,0:T(8,128)} %get-tuple-element.12), calls=%async_computation.1 | async-start | bytes 262144 | tf_op jit(solution)/shard_map/all_to_all | solution.py:348
  55.5 5.9 %collective-permute-start.1 = (f32[16,8,256]{2,1,0:T(8,128)S(1)}, f32[16,8,256]{2,1,0:T(8,128)S(1)}, u32[]{:S(2)}, u32[]{:S(2)}) collective-permute-start(f32[16,8,256]{2,1,0:T(8,128)S(1)} %slice.4), channel_id=1, source_target_pairs={{0,16},{16,0},{32,48},{48,32},{64,80},{80,64},{96,112},{112,96},{1... | collective-permute-start | bytes 393224 | tf_op jit(solution)/shard_map/ppermute | solution.py:351
  64.7 1.2 %collective-permute-start.2 = (f32[1,256]{1,0:T(1,128)S(1)}, f32[1,256]{1,0:T(1,128)S(1)}, u32[]{:S(2)}, u32[]{:S(2)}) collective-permute-start(f32[1,256]{1,0:T(1,128)S(1)} %get-tuple-element.18), channel_id=1, source_target_pairs={{0,16},{16,0},{32,48},{48,32},{64,80},{80,64},{96,112},{112,96},{1... | collective-permute-start | bytes 3080 | tf_op jit(solution)/shard_map/ppermute | solution.py:354

commit v10 on v9

--- a/solution.py
+++ b/solution.py
@@ -351,13 +351,23 @@
     other = lax.ppermute(packed[:, : parts.shape[1]], "row", swap)
     own, change = first_half(packed, gram_c)
     solved, squares = solve(core, own, change, packed, other, gram_c)
-    squares = squares + lax.ppermute(squares, "row", swap)
-    same_core = [
-        [(2 * chip + core) * n_col + c for chip in range(chips) for c in range(n_col)]
-        for core in range(2)
+    beside_x = [(i, i ^ 1) for i in range(n_col)]
+    across = [((i * n_col) + j, (i ^ 1) * n_col + (j ^ 1)) for i in range(n_row) for j in range(n_col)]
+    chip = squares + lax.ppermute(squares, "row", swap)
+    neighbour = lax.ppermute(squares, "col", beside_x) + lax.ppermute(squares, both, across)
+    squares = chip + neighbour
+    group = [
+        [
+            (2 * pair + which) * n_col + c
+            for pair in range(chips)
+            for c in range(n_col)
+            if c % 4 in ends
+        ]
+        for which in range(2)
+        for ends in ((0, 3), (1, 2))
     ]
-    copies = jnp.broadcast_to(squares[None], (chips * n_col,) + squares.shape)
-    squares = lax.all_to_all(copies, both, 0, 0, axis_index_groups=same_core)
+    copies = jnp.broadcast_to(squares[None], (len(group[0]),) + squares.shape)
+    squares = lax.all_to_all(copies, both, 0, 0, axis_index_groups=group)
     factor_a, col_scale = finish(squares, solved, rows_i * n_row)
     return (factor_a, col_scale[0])
 

time: 84.7 us -> 84.8 us (level)
  starting transfers between devices: 10.5 us -> 12.6 us
  blocking collectives: 54.3 us -> 52.2 us
    all_to_all x1, blocking collectives: 17.6 us -> 15.4 us  [local(): squares = lax.all_to_all(copies, both, 0, 0, axis_index_groups=group)]
    ppermute x1 -> x3, starting transfers between devices: 0.1 us -> 2.22 us  [the longest x1 1.35 us: local(): lax.ppermute(squares, 'col', beside_x) + lax.ppermute(squares, both, across)]
  transfers between devices with their start and end apart: 4 -> 6, of which waited for: 3 -> 3; matrix products, arithmetic and copies ran while one was open for 0% -> 0% of each run, Pallas kernels for 11% -> 11%
where the time goes in v10:
time: 84.8 us; the launch traced here: 83.9 us
  blocking collectives  52.2 us (62%)
  Pallas kernels  13.9 us (16%)
  starting transfers between devices  12.6 us (15%)
  waiting for transfers between devices  3.77 us (4%)
    all_to_all x1, blocking collectives, local(): mine = lax.all_to_all(copies, 'row', 0, 0, axis_index_groups=same_core)  20.8 us
    all_to_all x1, blocking collectives, local(): packed = lax.all_to_all(pack(parts, terms), 'col', 0, 0)  16 us
    all_to_all x1, blocking collectives, local(): squares = lax.all_to_all(copies, both, 0, 0, axis_index_groups=group)  15.4 us
    pallas_call x1, Pallas kernels, mttkrp(): pl.pallas_call(mttkrp_kernel, out_shape=(jax.ShapeDtypeStruct((rows_i, ra...  5.55 us
    all_to_all x1, starting transfers between devices, local(): parts = lax.all_to_all(parts, 'col', 0, 0)  5.49 us
    pallas_call x1, Pallas kernels, solve(): pl.pallas_call(solve_kernel, out_shape=(jax.ShapeDtypeStruct((packed.shap...  3.29 us
    pallas_call x1, Pallas kernels, first_half(): pl.pallas_call(first_kernel, out_shape=(half, half), compiler_params=pltp...  3.08 us
    ppermute x1, starting transfers between devices, local(): other = lax.ppermute(packed[:, :parts.shape[1]], 'row', swap)  2.81 us
  transfers between devices with their start and end apart: 6, of which 3 were waited for; matrix products, arithmetic and copies ran while one was open for 0% of the time, Pallas kernels for 11%

profile of v10, /device:TPU:1, one launch (start us, length us, event | category | flops | bytes accessed | tf_op | source)
XLA Modules:
  0.0 83.9 jit_solution(3909754625958860940)
XLA Ops:
  0.6 0.7 broadcast_in_dim.18
  1.4 20.8 %all_to_all.20.mine_ref = f32[8,16,256]{2,1,0:T(8,128)S(1)} all-to-all(f32[8,16,256]{2,1,0:T(8,128)S(1)} %broadcast_in_dim.18), channel_id=1, replica_groups={{0,32,64,96,128,160,192,224},{16,48,80,112,144,176,208,240},{1,33,65,97..., dimensions={0} | all-to-all | bytes 262144 | tf_op jit(solution)/shard_map/all_to_all | solution.py:345
  22.1 2.1 %collective-permute-start = (f32[8,16,256]{2,1,0:T(8,128)S(1)}, f32[8,16,256]{2,1,0:T(8,128)S(1)}, u32[]{:S(2)}, u32[]{:S(2)}) collective-permute-start(f32[8,16,256]{2,1,0:T(8,128)S(1)} %all_to_all.20.mine_ref), channel_id=1, source_target_pairs={{0,16},{16,0},{32,48},{48,32},{64,80},{80,64},{96,112},{112,96},{1... | collective-permute-start | bytes 393224 | tf_op jit(solution)/shard_map/ppermute | solution.py:346
  24.2 0.3 gram_own.1.own_ref
  24.5 0.0 copy-start
  24.5 0.7 collective-permute-done.other_ref
  25.2 0.9 %gram_part.1 = (f32[256,256]{1,0:T(8,128)S(1)}, f32[16,8,256]{2,1,0:T(8,128)}) custom-call(f32[8,16,256]{2,1,0:T(8,128)S(1)} %all_to_all.20.mine_ref, f32[8,16,256]{2,1,0:T(8,128)S(1)} %collective-permute-done.other_ref, f32[128,128]{1,0:T(8,128)S(1)} %gram_own.1.own_ref), custom_call_target="tpu_custom_call" | custom-call | flops 10000000000 | bytes 524288 | tf_op jit(solution)/shard_map/gram_part/pallas_call | solution.py:56
  26.2 5.5 %all-to-all-start.1 = ((f32[16,8,256]{2,1,0:T(8,128)}), f32[16,8,256]{2,1,0:T(8,128)S(1)}, u32[]{:S(2)}, u32[]{:S(2)}) async-start(f32[16,8,256]{2,1,0:T(8,128)} %get-tuple-element.12), calls=%async_computation.1 | async-start | bytes 262144 | tf_op jit(solution)/shard_map/all_to_all | solution.py:348
  31.7 0.0 copy-done
  31.7 5.5 %mttkrp.1 = (f32[256,256]{1,0:T(8,128)S(1)}, f32[256,256]{1,0:T(8,128)S(1)}) custom-call(s32[1]{0:T(128)} %bitcast.core_ref, f32[32,256,256]{2,1,0:T(8,128)} %slab_hbm.1, f32[256,256]{1,0:T(8,128)S(1)} %get-tuple-element.13.block_ref, f32[32,256]{1,0:T(8,128)S(1)} %copy-done), custom_call_target="tpu_custom_call" | custom-call | flops 3221225472 | bytes 8388608 | tf_op jit(solution)/shard_map/mttkrp/pallas_call | solution.py:128
  37.2 2.2 %all-to-all-done.1.parts_ref = f32[16,8,256]{2,1,0:T(8,128)S(1)} async-done(((f32[16,8,256]{2,1,0:T(8,128)}), f32[16,8,256]{2,1,0:T(8,128)S(1)}, u32[]{:S(2)}, u32[]{:S(2)}) %all-to-all-start.1) | async-done | bytes 131104 | tf_op jit(solution)/shard_map/all_to_all | solution.py:348
  39.5 16.0 %all_to_all.21.packed_ref = f32[16,24,256]{2,1,0:T(8,128)S(1)} all-to-all(f32[16,24,256]{2,1,0:T(8,128)S(1)} %pack.1), channel_id=1, replica_groups=mesh['row'=16,'col'=16] {'col'}, dimensions={0} | all-to-all | bytes 786432 | tf_op jit(solution)/shard_map/all_to_all | solution.py:350
  55.5 2.8 %collective-permute-start.1 = (f32[16,8,256]{2,1,0:T(8,128)S(1)}, f32[16,8,256]{2,1,0:T(8,128)S(1)}, u32[]{:S(2)}, u32[]{:S(2)}) collective-permute-start(f32[16,8,256]{2,1,0:T(8,128)S(1)} %slice.4), channel_id=1, source_target_pairs={{0,16},{16,0},{32,48},{48,32},{64,80},{80,64},{96,112},{112,96},{1... | collective-permute-start | bytes 393224 | tf_op jit(solution)/shard_map/ppermute | solution.py:351
  58.3 3.1 %first_half.1 = (f32[128,256]{1,0:T(8,128)S(1)}, f32[128,256]{1,0:T(8,128)S(1)}) custom-call(f32[16,24,256]{2,1,0:T(8,128)S(1)} %all_to_all.21.packed_ref, f32[256,256]{1,0:T(8,128)S(1)} %get-tuple-element.15.gram_c_ref), custom_call_target="tpu_custom_call" | custom-call | flops 10000000000 | bytes 393216 | tf_op jit(solution)/shard_map/first_half/pallas_call | solution.py:272
  61.4 0.0 collective-permute-done.1.other_ref
  61.4 3.3 %solve.1 = (f32[16,256]{1,0:T(8,128)S(1)}, f32[1,256]{1,0:T(1,128)S(1)}) custom-call(s32[1]{0:T(128)} %bitcast.core_ref, f32[128,256]{1,0:T(8,128)S(1)} %get-tuple-element.16.own_ref, f32[128,256]{1,0:T(8,128)S(1)} %get-tuple-element.17.change_ref, f32[16,24,256]{2,1,0:T(8,128)S(1)} %all_to_all.21.packed_ref, ...), custom_call_target="tpu_custom_call" | custom-call | tf_op jit(solution)/shard_map/solve/pallas_call | solution.py:302
  64.7 0.1 collective-permute-start.4
  64.8 1.4 %collective-permute-start.3 = (f32[1,256]{1,0:T(1,128)S(1)}, f32[1,256]{1,0:T(1,128)S(1)}, u32[]{:S(2)}, u32[]{:S(2)}) collective-permute-start(f32[1,256]{1,0:T(1,128)S(1)} %get-tuple-element.18), channel_id=1, source_target_pairs={{0,1},{1,0},{2,3},{3,2},{4,5},{5,4},{6,7},{7,6},{8,9},{9,8},{10,11... | collective-permute-start | bytes 3080 | tf_op jit(solution)/shard_map/ppermute | solution.py:357
  66.1 0.8 collective-permute-start.2
  66.9 0.9 %collective-permute-done.4 = f32[1,256]{1,0:T(1,128)S(1)} collective-permute-done((f32[1,256]{1,0:T(1,128)S(1)}, f32[1,256]{1,0:T(1,128)S(1)}, u32[]{:S(2)}, u32[]{:S(2)}) %collective-permute-start.4) | collective-permute-done | bytes 1056 | tf_op jit(solution)/shard_map/ppermute | solution.py:357
  67.8 0.0 collective-permute-done.3
  67.8 0.0 collective-permute-done.2
  67.8 15.4 %all_to_all.22.squares_ref = f32[64,1,256]{2,1,0:T(1,128)S(1)} all-to-all(f32[64,1,256]{2,1,0:T(1,128)S(1)} %broadcast_in_dim.20), channel_id=1, replica_groups={{0,3,4,7,8,11,12,15,32,35,36,39,40,43,44,47,64,67,68,71,72,75,76,79,96,..., dimensions={0} | all-to-all | bytes 131072 | tf_op jit(solution)/shard_map/all_to_all | solution.py:370
  83.2 0.7 finish.1
  (4 shorter events, 0.1 us)
Async XLA Ops:
  22.1 3.1 %collective-permute-start = (f32[8,16,256]{2,1,0:T(8,128)S(1)}, f32[8,16,256]{2,1,0:T(8,128)S(1)}, u32[]{:S(2)}, u32[]{:S(2)}) collective-permute-start(f32[8,16,256]{2,1,0:T(8,128)S(1)} %all_to_all.20.mine_ref), channel_id=1, source_target_pairs={{0,16},{16,0},{32,48},{48,32},{64,80},{80,64},{96,112},{112,96},{1... | collective-permute-start | bytes 393224 | tf_op jit(solution)/shard_map/ppermute | solution.py:346
  24.5 7.1 %copy-start = (f32[32,256]{1,0:T(8,128)S(1)}, f32[32,256]{1,0:T(8,128)}, u32[]{:S(2)}) copy-start(f32[32,256]{1,0:T(8,128)} %c_ref.1) | copy-start | bytes 98308
  26.2 13.3 %all-to-all-start.1 = ((f32[16,8,256]{2,1,0:T(8,128)}), f32[16,8,256]{2,1,0:T(8,128)S(1)}, u32[]{:S(2)}, u32[]{:S(2)}) async-start(f32[16,8,256]{2,1,0:T(8,128)} %get-tuple-element.12), calls=%async_computation.1 | async-start | bytes 262144 | tf_op jit(solution)/shard_map/all_to_all | solution.py:348
  55.5 5.9 %collective-permute-start.1 = (f32[16,8,256]{2,1,0:T(8,128)S(1)}, f32[16,8,256]{2,1,0:T(8,128)S(1)}, u32[]{:S(2)}, u32[]{:S(2)}) collective-permute-start(f32[16,8,256]{2,1,0:T(8,128)S(1)} %slice.4), channel_id=1, source_target_pairs={{0,16},{16,0},{32,48},{48,32},{64,80},{80,64},{96,112},{112,96},{1... | collective-permute-start | bytes 393224 | tf_op jit(solution)/shard_map/ppermute | solution.py:351
  64.7 3.1 %collective-permute-start.4 = (f32[1,256]{1,0:T(1,128)S(1)}, f32[1,256]{1,0:T(1,128)S(1)}, u32[]{:S(2)}, u32[]{:S(2)}) collective-permute-start(f32[1,256]{1,0:T(1,128)S(1)} %get-tuple-element.18), channel_id=1, source_target_pairs={{0,17},{1,16},{2,19},{3,18},{4,21},{5,20},{6,23},{7,22},{8,25},{9,... | collective-permute-start | bytes 3080 | tf_op jit(solution)/shard_map/ppermute | solution.py:357
  64.8 3.0 %collective-permute-start.3 = (f32[1,256]{1,0:T(1,128)S(1)}, f32[1,256]{1,0:T(1,128)S(1)}, u32[]{:S(2)}, u32[]{:S(2)}) collective-permute-start(f32[1,256]{1,0:T(1,128)S(1)} %get-tuple-element.18), channel_id=1, source_target_pairs={{0,1},{1,0},{2,3},{3,2},{4,5},{5,4},{6,7},{7,6},{8,9},{9,8},{10,11... | collective-permute-start | bytes 3080 | tf_op jit(solution)/shard_map/ppermute | solution.py:357
  66.1 1.6 %collective-permute-start.2 = (f32[1,256]{1,0:T(1,128)S(1)}, f32[1,256]{1,0:T(1,128)S(1)}, u32[]{:S(2)}, u32[]{:S(2)}) collective-permute-start(f32[1,256]{1,0:T(1,128)S(1)} %get-tuple-element.18), channel_id=1, source_target_pairs={{0,16},{16,0},{32,48},{48,32},{64,80},{80,64},{96,112},{112,96},{1... | collective-permute-start | bytes 3080 | tf_op jit(solution)/shard_map/ppermute | solution.py:356
